TPU v7x, 32 devices: a whole 2x2x4 slice. The times are simulated.
32 devices in a mesh: row: 8 (over y, x, core), col: 4 (over z).
Axes of the slice: x: 2, y: 2, z: 4, core: 2. Of those that a mesh axis runs over, the one named last changes fastest.
Arguments:
- waveform: bfloat16 [32, 1024, 8192], P(('row', 'col')), may hold values from -50 to 50, as said below
- valid_mask: int32 [32, 1024], P(('row', 'col')), may hold values 0 or 1
- band_starts: int32 [10], replicated, may hold values from 0 to 4080
- station_map: int32 [1024], replicated, may hold values from 0 to 1023, each once
Outputs:
- stacked: bfloat16 [2, 160, 1024, 1024], P(None, None, 'row', 'col')
Inputs may be any that keep to these rules, and one draw needn't show every extreme that they name: `waveform`: entries are real samples whose per-trace scale varies from trace to trace. `band_starts`: each band's 16 bins lie below 4096. `station_map`: a permutation of the stations.
All inputs are finite; a program needn't handle non-finite values. No bound on the sum of `valid_mask` on one device may be relied on, other than what follows from the above.
Results may differ from a plain program's by a relative error of at most 0.0068.
Values may be sent and summed in bfloat16 or wider, within the bound.
A program may use at most 128 MiB of HBM per device.

v0:
```python
import math

import jax
import jax.numpy as jnp
from jax import lax
from jax.sharding import PartitionSpec as P

BINS = 16


def make_table(band_starts, length, bin_count):
    frequency = (band_starts[:, None] + jnp.arange(bin_count, dtype=jnp.int32)[None, :]).reshape(-1)
    samples = jnp.arange(length, dtype=jnp.int32)
    phase_index = frequency[:, None] * samples[None, :] % length
    angles = phase_index.astype(jnp.float32) * jnp.float32(2.0 * math.pi / length)
    scaling = jnp.float32(length ** (-0.5))
    return (jnp.concatenate([jnp.cos(angles), -jnp.sin(angles)], axis=0) * scaling).astype(
        jnp.bfloat16
    )


def whiten(spectra, mask_rows, band_count):
    count, double_bins, stations = spectra.shape
    half = double_bins // 2
    real_part = spectra[:, :half]
    imag_part = spectra[:, half:]
    power_bins = real_part * real_part + imag_part * imag_part
    band_mean = power_bins.reshape(count, band_count, half // band_count, stations).mean(
        axis=2, keepdims=True
    )
    band_mean = jnp.broadcast_to(
        band_mean, (count, band_count, half // band_count, stations)
    ).reshape(count, half, stations)
    factor = mask_rows[:, None, :].astype(jnp.float32) / jnp.sqrt(power_bins + band_mean + 0.1)
    return jnp.concatenate([real_part * factor, imag_part * factor], axis=1).astype(jnp.bfloat16)


def pair_product(left, right):
    return jnp.einsum("wfa,wfb->fab", left, right, preferred_element_type=jnp.float32)


def cross_spectra(left, right):
    half = left.shape[1] // 2
    real_left, imag_left = (left[:, :half], left[:, half:])
    real_right, imag_right = (right[:, :half], right[:, half:])
    real_out = pair_product(real_left, real_right) + pair_product(imag_left, imag_right)
    imag_out = pair_product(real_left, imag_right) - pair_product(imag_left, real_right)
    return jnp.stack([real_out, imag_out], axis=0)


def body(waveform, valid_mask, band_starts, station_map):
    length = waveform.shape[2]
    dft_table = make_table(band_starts, length, BINS)
    spectra = jnp.einsum("fl,wsl->wfs", dft_table, waveform, preferred_element_type=jnp.float32)
    sum_squares = jnp.einsum("wsl,wsl->ws", waveform, waveform, preferred_element_type=jnp.float32)
    rms_value = jnp.sqrt(sum_squares / length + 1e-06)
    spectra = spectra / rms_value[:, None, :]
    whitened = whiten(spectra, valid_mask, band_starts.shape[0])
    row_count = lax.axis_size("row")
    col_count = lax.axis_size("col")
    stations = whitened.shape[2]
    shard_width = stations // (row_count * col_count)
    positions = jnp.arange(stations, dtype=jnp.int32)
    shard_number = positions // shard_width
    offset_inside = positions % shard_width
    col_order = (
        shard_number % col_count * (stations // col_count)
        + shard_number // col_count * shard_width
        + offset_inside
    )
    row_source = jnp.take(whitened, station_map, axis=2)
    col_source = jnp.take(whitened, jnp.take(station_map, col_order), axis=2)
    row_local, col_local = (
        lax.all_to_all(row_source, ("row", "col"), split_axis=2, concat_axis=0, tiled=True),
        lax.all_to_all(col_source, ("row", "col"), split_axis=2, concat_axis=0, tiled=True),
    )
    row_block = lax.all_gather(row_local, "col", axis=2, tiled=True)
    scaling = jnp.float32(float(row_block.shape[0]) ** (-0.5))
    col_block = lax.all_gather(col_local, "row", axis=2, tiled=True)
    stacked = cross_spectra(row_block, col_block)
    return (stacked * scaling).astype(jnp.bfloat16)


def solution(mesh):
    placed = (P(("row", "col"), None, None), P(("row", "col"), None), P(), P())
    return jax.shard_map(
        body, mesh=mesh, in_specs=placed, out_specs=P(None, None, "row", "col"), check_vma=False
    )
```

profile of v0, /device:TPU:0, one launch (start us, length us, event | category | flops | bytes accessed | tf_op | source)
XLA Modules:
  0.0 311.6 jit_solution(16157527892206446559)
XLA Ops:
  6.5 0.7 compare_and_fusion.1
  7.2 0.7 fusion.57
  7.9 0.7 convert_element_type.31
  8.6 7.2 %fusion.1 = f32[1024]{0:T(1024)S(1)} fusion(bf16[1,1024,8192]{2,1,0:T(8,128)(2,1)} %param.6), kind=kLoop, calls=%fused_computation.6 | loop fusion | flops 25164800 | bytes 16781312 | tf_op jit(solution)/shard_map/wsl,wsl->ws/dot_general | solution.py:55
  16.0 23.5 %fusion.19 = (f32[160,8192]{1,0:T(8,128)}, f32[160,8192]{1,0:T(8,128)}) fusion(s32[160]{0:T(256)S(1)} %add.158), kind=kLoop, calls=%fused_computation.30 | loop fusion | flops 19660800 | bytes 10486400 | tf_op jit(solution)/shard_map/cos | solution.py:17
  39.5 12.2 %divide_bitcast_fusion = f32[1,320,1024]{2,1,0:T(8,128)S(1)} fusion(bf16[1,1024,8192]{2,1,0:T(8,128)(2,1)} %param.6, f32[160,8192]{1,0:T(8,128)} %get-tuple-element.11, f32[160,8192]{1,0:T(8,128)} %get-tuple-element.10, f32[1024]{0:T(1024)S(1)} %add_sqrt_fusion), kind=kOutput, calls=%fused_computation.36 | convolution fusion | flops 5376901120 | bytes 28577792 | tf_op jit(solution)/shard_map/fl,wsl->wfs/dot_general | solution.py:54
  52.4 0.4 copy.13
  52.8 4.4 %gather_fusion.1 = bf16[1024,320]{1,0:T(8,128)(2,1)S(1)} fusion(bf16[320,1024]{0,1:T(8,128)(2,1)S(1)} %copy.13, s32[1024]{0:T(1024)S(1)} %fusion.57), kind=kCustom, calls=%fused_computation.clone | custom fusion | bytes 1314816 | tf_op jit(solution)/shard_map/jit(_take)/gather | solution.py:71
  57.4 1.2 copy.30
  58.7 0.5 broadcast.314
  59.2 5.6 %reduce.3 = bf16[1024,320]{1,0:T(8,128)(2,1)S(1)} reduce(bf16[1024,1,320]{2,1,0:T(2,128)(2,1)S(1)} %bitcast.71, bf16[]{:T(256)} %broadcast.314), dimensions={1}, to_apply=%bitcast.69.reduce_sub_computation | reduce | bytes 1310722
  64.8 0.8 reshape.300
  65.6 24.0 %all_to_all.36 = bf16[32,2,5120]{2,1,0:T(2,128)(2,1)S(1)} all-to-all(bf16[32,2,5120]{2,1,0:T(2,128)(2,1)S(1)} %reshape.300), channel_id=1, replica_groups=mesh['row'=8,'col'=4] {'row','col'}, dimensions={0} | all-to-all | bytes 1310720 | tf_op jit(solution)/shard_map/all_to_all | solution.py:74
  89.6 1.4 reshape.301
  91.2 1.1 copy.15
  92.4 4.7 %gather_fusion = s32[1024]{0:T(1024)S(1)} fusion(s32[1024]{0:T(1024)S(1)} %copy-done, s32[1024]{0:T(1024)S(1)} %broadcast_clamp_fusion.1), kind=kCustom, calls=%fused_computation.2 | custom fusion | bytes 12288 | tf_op jit(solution)/shard_map/jit(_take)/gather | solution.py:72
  97.2 3.9 %gather_fusion.2 = bf16[1024,320]{1,0:T(8,128)(2,1)S(1)} fusion(bf16[320,1024]{0,1:T(8,128)(2,1)S(1)} %copy.13, s32[1024]{0:T(1024)S(1)} %broadcast_clamp_fusion), kind=kCustom, calls=%fused_computation.1.clone | custom fusion | bytes 1314816 | tf_op jit(solution)/shard_map/jit(_take)/gather | solution.py:72
  101.3 1.2 copy.29
  102.5 5.6 %reduce.4 = bf16[1024,320]{1,0:T(8,128)(2,1)S(1)} reduce(bf16[1024,1,320]{2,1,0:T(2,128)(2,1)S(1)} %bitcast.72, bf16[]{:T(256)} %broadcast.314), dimensions={1}, to_apply=%bitcast.68.reduce_sub_computation | reduce | bytes 1310722
  108.2 0.8 reshape.302
  109.0 38.7 %all_to_all.37 = bf16[32,2,5120]{2,1,0:T(2,128)(2,1)S(1)} all-to-all(bf16[32,2,5120]{2,1,0:T(2,128)(2,1)S(1)} %reshape.302), channel_id=1, replica_groups=mesh['row'=8,'col'=4] {'row','col'}, dimensions={0} | all-to-all | bytes 1310720 | tf_op jit(solution)/shard_map/all_to_all | solution.py:75
  147.7 1.4 reshape.303
  149.3 1.2 copy.19
  150.4 19.0 %all-gather.5.cloned.1.call-done = bf16[32,1,320,128]{2,0,1,3:T(8,128)(2,1)} async-done(((bf16[32,1,320,32]{2,0,1,3:T(8,128)(2,1)}), bf16[32,1,320,128]{2,0,1,3:T(8,128)(2,1)}) %all-gather.5.cloned.1.call-update) | async-done | bytes 2621456 | tf_op jit(solution)/shard_map/all_gather | solution.py:77
  169.4 4.5 %copy.16 = bf16[32,1,320,128]{3,0,2,1:T(8,128)(2,1)S(1)} copy(bf16[32,1,320,128]{2,0,1,3:T(8,128)(2,1)} %all-gather.5.cloned.1.call-done) | data formatting | bytes 5242880 | tf_op jit(solution)/shard_map/all_gather | solution.py:77
  173.9 41.5 %all-gather.7.cloned.1.call-done = bf16[32,1,320,256]{2,0,1,3:T(8,128)(2,1)} async-done(((bf16[32,1,320,32]{2,0,1,3:T(8,128)(2,1)}), bf16[32,1,320,256]{2,0,1,3:T(8,128)(2,1)}) %all-gather.7.cloned.1.call-update) | async-done | bytes 5242896 | tf_op jit(solution)/shard_map/all_gather | solution.py:79
  215.4 9.4 %copy.20 = bf16[32,1,320,256]{3,0,2,1:T(8,128)(2,1)} copy(bf16[32,1,320,256]{2,0,1,3:T(8,128)(2,1)} %all-gather.7.cloned.1.call-done) | data formatting | bytes 10485760 | tf_op jit(solution)/shard_map/all_gather | solution.py:79
  224.9 12.4 %fusion.17 = f32[160,128,256]{2,1,0:T(8,128)} fusion(bf16[32,1,320,128]{3,0,2,1:T(8,128)(2,1)S(1)} %copy.16, bf16[32,320,256]{2,0,1:T(8,128)(2,1)} %bitcast.75), kind=kOutput, calls=%fused_computation.28 | convolution fusion | flops 335544320 | bytes 26214400 | tf_op jit(solution)/shard_map/wfa,wfb->fab/dot_general | solution.py:39
  237.2 8.9 %fusion.14 = f32[160,128,256]{2,1,0:T(8,128)} fusion(bf16[32,1,320,128]{3,0,2,1:T(8,128)(2,1)S(1)} %copy.16, bf16[32,320,256]{2,0,1:T(8,128)(2,1)S(1)} %bitcast.78), kind=kOutput, calls=%fused_computation.25 | convolution fusion | flops 335544320 | bytes 26214400 | tf_op jit(solution)/shard_map/wfa,wfb->fab/dot_general | solution.py:39
  246.2 17.7 %subtract_bitcast_fusion = f32[1,160,128,256]{3,2,1,0:T(8,128)} fusion(f32[160,128,256]{2,1,0:T(8,128)} %fusion.17, bf16[32,1,320,128]{3,0,2,1:T(8,128)(2,1)S(1)} %copy.16, bf16[32,320,256]{2,0,1:T(8,128)(2,1)} %bitcast.76), kind=kOutput, calls=%fused_computation.7 | convolution fusion | flops 340787200 | bytes 47185920 | tf_op jit(solution)/shard_map/wfa,wfb->fab/dot_general | solution.py:39
  263.8 17.7 %add_bitcast_fusion = f32[1,160,128,256]{3,2,1,0:T(8,128)} fusion(f32[160,128,256]{2,1,0:T(8,128)} %fusion.14, bf16[32,1,320,128]{3,0,2,1:T(8,128)(2,1)S(1)} %copy.16, bf16[32,320,256]{2,0,1:T(8,128)(2,1)} %bitcast.77), kind=kOutput, calls=%fused_computation.8 | convolution fusion | flops 340787200 | bytes 47185920 | tf_op jit(solution)/shard_map/wfa,wfb->fab/dot_general | solution.py:39
  281.5 23.0 %fusion = bf16[2,160,128,256]{3,2,1,0:T(8,128)(2,1)} fusion(f32[1,160,128,256]{3,2,1,0:T(8,128)} %subtract_bitcast_fusion, f32[1,160,128,256]{3,2,1,0:T(8,128)} %add_bitcast_fusion), kind=kLoop, calls=%fused_computation.4 | loop fusion | flops 31457280 | bytes 62914560 | tf_op jit(solution)/shard_map/convert_element_type | solution.py:81
  (27 shorter events, 1.6 us)
Async XLA Ops:
  6.5 162.9 %all-gather.5.cloned.1.call-start = ((), (), s32[]{:S(2)}) async-start(), calls=%async_computation.2 | async-start | bytes 3932160 | tf_op jit(solution)/shard_map/all_gather | solution.py:77
  8.6 7.2 %copy-start.2 = (s32[10]{0:T(128)S(1)}, s32[10]{0:T(128)}, u32[]{:S(2)}) copy-start(s32[10]{0:T(128)} %param.8) | copy-start | bytes 124
  64.8 27.6 %copy-start = (s32[1024]{0:T(1024)S(1)}, s32[1024]{0:T(1024)}, u32[]{:S(2)}) copy-start(s32[1024]{0:T(1024)} %param.9) | copy-start | bytes 12292
  92.3 123.1 %all-gather.7.cloned.1.call-start = ((), (), s32[]{:S(2)}) async-start(), calls=%async_computation.3 | async-start | bytes 7077888 | tf_op jit(solution)/shard_map/all_gather | solution.py:79
  224.9 12.4 %copy-start.1 = (bf16[32,1,320,256]{3,0,2,1:T(8,128)(2,1)S(1)}, bf16[32,1,320,256]{3,0,2,1:T(8,128)(2,1)}, u32[]{:S(2)}) copy-start(bf16[32,1,320,256]{3,0,2,1:T(8,128)(2,1)} %copy.20) | copy-start | bytes 15728644
Sparse Core Ops, SparseCore 0:
  92.4 76.9 all-gather.4
  171.3 44.0 all-gather.6
where the time goes:
time: 317 us; the launch traced here: 312 us
  matrix products  68.9 us (22%)
  other arithmetic  68.1 us (21%)
  blocking collectives  62.8 us (20%)
  waiting for transfers between devices  60.5 us (19%)
  local copies, waits for them, and re-layouts  37.4 us (12%)
  between operations  13.9 us (4%)
    dot_general x4, matrix products, pair_product(): jnp.einsum('wfa,wfb->fab', left, right, preferred_element_type=jnp.float32)  56.6 us
    all_gather x1, waiting for transfers between devices, body(): col_block = lax.all_gather(col_local, 'row', axis=2, tiled=True)  41.5 us
    all_to_all x1, blocking collectives, body(): lax.all_to_all(col_source, ('row', 'col'), split_axis=2, concat_axis=0, t...  38.7 us
    all_to_all x1, blocking collectives, body(): lax.all_to_all(row_source, ('row', 'col'), split_axis=2, concat_axis=0, t...  24 us
    cos x1, other arithmetic, make_table(): jnp.cos(angles)  23.5 us
    convert_element_type x1, other arithmetic, body(): return (stacked * scaling).astype(jnp.bfloat16)  23 us
    all_gather x1, waiting for transfers between devices, body(): row_block = lax.all_gather(row_local, 'col', axis=2, tiled=True)  19 us
    dot_general x1, matrix products, body(): jnp.einsum('fl,wsl->wfs', dft_table, waveform, preferred_element_type=jnp...  12.2 us
  transfers between devices with their start and end apart: 2, of which 2 were waited for; matrix products, arithmetic and copies ran while one was open for 8% of the time, Pallas kernels for 0%

commit v1 on v0

v1 whole, which is shorter than its diff:
```python
import functools
import math

import jax
import jax.numpy as jnp
from jax import lax
from jax.experimental import pallas as pl
from jax.experimental.pallas import tpu as pltpu
from jax.sharding import PartitionSpec as P

BINS = 16
CHUNK = 1024
MESH = pl.DeviceIdType.MESH


def phase_tables(band_starts, length):
    frequency = (band_starts[:, None] + jnp.arange(BINS, dtype=jnp.int32)[None, :]).reshape(-1)

    def parts(samples):
        phase = frequency[:, None] * samples[None, :] % length
        angles = phase.astype(jnp.float32) * jnp.float32(2.0 * math.pi / length)
        return jnp.cos(angles), jnp.sin(angles)

    fine = parts(jnp.arange(CHUNK, dtype=jnp.int32))
    coarse = parts(jnp.arange(128, dtype=jnp.int32) * CHUNK)
    scaling = jnp.float32(length ** (-0.5))
    return fine + (coarse[0] * scaling, coarse[1] * scaling)


def spectra_kernel(
    length, wave, fine_cos, fine_sin, coarse_cos, coarse_sin, mask, order, out, acc, squares, white
):
    step = pl.program_id(0)
    stations = wave.shape[1]
    double_bins = acc.shape[0]
    bands = double_bins // (2 * BINS)

    @pl.when(step == 0)
    def _():
        acc[...] = jnp.zeros_like(acc)
        squares[...] = jnp.zeros_like(squares)

    lane = lax.broadcasted_iota(jnp.int32, coarse_cos.shape, 1)
    first_cos = jnp.sum(jnp.where(lane == step, coarse_cos[...], 0.0), axis=1, keepdims=True)
    first_sin = jnp.sum(jnp.where(lane == step, coarse_sin[...], 0.0), axis=1, keepdims=True)
    real = (first_cos * fine_cos[...] - first_sin * fine_sin[...]).astype(jnp.bfloat16)
    imag = (-(first_sin * fine_cos[...]) - first_cos * fine_sin[...]).astype(jnp.bfloat16)
    table = jnp.concatenate(
        [real.reshape(bands, BINS, CHUNK), imag.reshape(bands, BINS, CHUNK)], axis=1
    ).reshape(double_bins, CHUNK)
    acc[...] += lax.dot_general(
        table, wave[0], (((1,), (1,)), ((), ())), preferred_element_type=jnp.float32
    )
    total = squares[...]
    for tile in range(CHUNK // 128):
        part = wave[0, :, tile * 128 : (tile + 1) * 128].astype(jnp.float32)
        total = total + part * part
    squares[...] = total

    @pl.when(step == pl.num_programs(0) - 1)
    def _():
        ones = jnp.ones((8, 128), jnp.float32)
        sums = lax.dot_general(
            ones,
            squares[...],
            (((1,), (1,)), ((), ())),
            precision=lax.Precision.HIGHEST,
            preferred_element_type=jnp.float32,
        )[0:1]
        inverse = 1.0 / jnp.sqrt(sums / length + 1e-06)
        valid = mask[...].astype(jnp.float32)
        for band in range(bands):
            top = band * 2 * BINS
            re = acc[top : top + BINS, :] * inverse
            im = acc[top + BINS : top + 2 * BINS, :] * inverse
            power = re * re + im * im
            mean = jnp.mean(power, axis=0, keepdims=True)
            factor = valid / jnp.sqrt(power + mean + 0.1)
            white[top : top + BINS, :] = (re * factor).astype(jnp.bfloat16)
            white[top + BINS : top + 2 * BINS, :] = (im * factor).astype(jnp.bfloat16)
        blocks, _, width = out.shape
        group = 256
        for start in range(0, stations, group):
            source = lax.broadcasted_iota(jnp.int32, (stations, group), 0)
            pick = (source == order[0:1, start : start + group]).astype(jnp.float32)
            placed = jnp.dot(
                white[...], pick.astype(jnp.bfloat16), preferred_element_type=jnp.float32
            ).astype(jnp.bfloat16)
            for inner in range(group // width):
                out[start // width + inner] = placed[:, inner * width : (inner + 1) * width]


def exchange_kernel(
    rows, cols, white, row_all, col_all,
    local_sem, row_sent, row_got, col_sent, col_got,
    right_sent, right_got, left_sent, left_got, chip_sent, chip_got, pair_sent, pair_got,
):
    r = lax.axis_index("row")
    c = lax.axis_index("col")
    chips = rows // 2
    core = lax.rem(r, 2)
    chip = r // 2
    twin = r + 1 - 2 * core
    per = rows // cols

    barrier = pltpu.get_barrier_semaphore()
    for d in range(1, rows):
        pl.semaphore_signal(
            barrier, inc=1, device_id=(lax.rem(r + d, rows), c), device_id_type=MESH
        )
    for d in range(1, cols):
        pl.semaphore_signal(
            barrier, inc=1, device_id=(r, lax.rem(c + d, cols)), device_id_type=MESH
        )
    pl.semaphore_wait(barrier, rows - 1 + cols - 1)

    def remote(src, dst, sent, got, target):
        return pltpu.make_async_remote_copy(
            src_ref=src, dst_ref=dst, send_sem=sent, recv_sem=got,
            device_id=target, device_id_type=MESH,
        )

    def col_part(block):
        return white.at[pl.ds(block * per, per)]

    col_first = []
    for d in range(1, cols):
        other = lax.rem(c + d, cols)
        col_first.append(
            remote(col_part(other), col_all.at[c, r], col_sent.at[d], col_got.at[d], (r, other))
        )
        col_first[-1].start()
    row_first = []
    for d in range(1, rows):
        other = lax.rem(r + d, rows)
        row_first.append(
            remote(white.at[other], row_all.at[c, r], row_sent.at[d], row_got.at[d], (other, c))
        )
        row_first[-1].start()
    own_row = pltpu.make_async_copy(white.at[r], row_all.at[c, r], local_sem.at[0])
    own_row.start()
    own_col = pltpu.make_async_copy(col_part(c), col_all.at[c, r], local_sem.at[1])
    own_col.start()

    for d in range(1, rows):
        other = lax.rem(r + rows - d, rows)
        remote(
            white.at[r], row_all.at[c, other], row_sent.at[d], row_got.at[d], (other, c)
        ).wait_recv()
    own_row.wait()

    def to_right(step):
        block = c - step
        return remote(
            row_all.at[block], row_all.at[block],
            right_sent.at[step], right_got.at[step], (r, c + 1),
        )

    def to_left(step):
        block = c + step
        return remote(
            row_all.at[block], row_all.at[block],
            left_sent.at[step], left_got.at[step], (r, c - 1),
        )

    def from_left(step):
        block = c - 1 - step
        return remote(
            row_all.at[block], row_all.at[block],
            right_sent.at[step], right_got.at[step], (r, c - 1),
        )

    def from_right(step):
        block = c + 1 + step
        return remote(
            row_all.at[block], row_all.at[block],
            left_sent.at[step], left_got.at[step], (r, c + 1),
        )

    def sends(step, act):
        @pl.when((c + 1 < cols) & (c - step >= 0))
        def _():
            act(to_right(step))

        @pl.when((c - 1 >= 0) & (c + step < cols))
        def _():
            act(to_left(step))

    def receives(step):
        @pl.when(c - 1 - step >= 0)
        def _():
            from_left(step).wait_recv()

        @pl.when(c + 1 + step < cols)
        def _():
            from_right(step).wait_recv()

    sends(0, lambda copy: copy.start())

    for d in range(1, cols):
        other = lax.rem(c + cols - d, cols)
        remote(
            col_part(c), col_all.at[other, r], col_sent.at[d], col_got.at[d], (r, other)
        ).wait_recv()
    own_col.wait()

    def to_chip(d):
        other = 2 * lax.rem(chip + d, chips) + core
        return remote(
            col_all.at[:, r], col_all.at[:, r], chip_sent.at[d], chip_got.at[d], (other, c)
        )

    def from_chip(d):
        other = 2 * lax.rem(chip + chips - d, chips) + core
        return remote(
            col_all.at[:, other], col_all.at[:, other],
            chip_sent.at[d], chip_got.at[d], (other, c),
        )

    def to_twin(d):
        source = 2 * lax.rem(chip + chips - d, chips) + core
        return remote(
            col_all.at[:, source], col_all.at[:, source],
            pair_sent.at[d], pair_got.at[d], (twin, c),
        )

    def from_twin(d):
        source = 2 * lax.rem(chip + chips - d, chips) + 1 - core
        return remote(
            col_all.at[:, source], col_all.at[:, source],
            pair_sent.at[d], pair_got.at[d], (twin, c),
        )

    for d in range(1, chips):
        to_chip(d).start()
    to_twin(0).start()

    for step in range(max(cols - 1, chips - 1)):
        if step < cols - 1:
            receives(step)
            if step + 1 < cols - 1:
                sends(step + 1, lambda copy: copy.start())
        if step + 1 < chips:
            from_chip(step + 1).wait_recv()
            to_twin(step + 1).start()
    for d in range(chips):
        from_twin(d).wait_recv()
    for copy in col_first + row_first:
        copy.wait_send()
    for step in range(cols - 1):
        sends(step, lambda copy: copy.wait_send())
    for d in range(1, chips):
        to_chip(d).wait_send()
    for d in range(chips):
        to_twin(d).wait_send()


def pairs_kernel(scaling, row_block, col_block, out, spread):
    windows, depth, width = row_block.shape
    per = col_block.shape[1]
    for window in range(windows):
        lines = pl.ds(window * depth, depth)
        spread[0, lines, 0:width] = row_block[window].astype(jnp.float32)
        for part in range(per):
            spread[1 + part, lines, 0:width] = col_block[window, part].astype(jnp.float32)

    def pick(plane, line):
        picked = spread[plane, pl.ds(line, windows, stride=depth), :]
        return picked[:, 0:width].astype(jnp.bfloat16)

    for bin_ in range(BINS):
        left = jnp.concatenate([pick(0, bin_), pick(0, BINS + bin_)], axis=0)
        real = jnp.concatenate([pick(1 + part, bin_) for part in range(per)], axis=1)
        imag = jnp.concatenate([pick(1 + part, BINS + bin_) for part in range(per)], axis=1)
        right = jnp.concatenate(
            [jnp.concatenate([real, imag], axis=0), jnp.concatenate([imag, -real], axis=0)], axis=1
        )
        both = lax.dot_general(
            left, right, (((0,), (0,)), ((), ())), preferred_element_type=jnp.float32
        ) * scaling
        wide = per * width
        out[0, bin_] = both[:, 0:wide].astype(jnp.bfloat16)
        out[1, bin_] = both[:, wide : 2 * wide].astype(jnp.bfloat16)


def body(rows, cols, waveform, valid_mask, band_starts, station_map):
    _, stations, length = waveform.shape
    bands = band_starts.shape[0]
    double_bins = 2 * BINS * bands
    half = double_bins // 2
    width = stations // rows
    per = rows // cols
    windows = rows * cols
    steps = length // CHUNK
    whole = lambda shape: pl.BlockSpec(shape, lambda i: (0,) * len(shape))
    tables = phase_tables(band_starts, length)
    white = pl.pallas_call(
        functools.partial(spectra_kernel, length),
        grid=(steps,),
        out_shape=jax.ShapeDtypeStruct((rows, double_bins, width), jnp.bfloat16),
        in_specs=[
            pl.BlockSpec((1, stations, CHUNK), lambda i: (0, 0, i)),
            whole((half, CHUNK)),
            whole((half, CHUNK)),
            whole((half, 128)),
            whole((half, 128)),
            whole((1, stations)),
            whole((1, stations)),
        ],
        out_specs=whole((rows, double_bins, width)),
        scratch_shapes=[
            pltpu.VMEM((double_bins, stations), jnp.float32),
            pltpu.VMEM((stations, 128), jnp.float32),
            pltpu.VMEM((double_bins, stations), jnp.bfloat16),
        ],
        compiler_params=pltpu.CompilerParams(vmem_limit_bytes=48 * 1024 * 1024),
        name="spectra",
    )(waveform, *tables, valid_mask, station_map[None, :])

    dma = pltpu.SemaphoreType.DMA
    chips = rows // 2
    row_all, col_all = pl.pallas_call(
        functools.partial(exchange_kernel, rows, cols),
        out_shape=[
            jax.ShapeDtypeStruct((cols, rows, double_bins, width), jnp.bfloat16),
            jax.ShapeDtypeStruct((cols, rows, per, double_bins, width), jnp.bfloat16),
        ],
        in_specs=[pl.BlockSpec(memory_space=pl.ANY)],
        out_specs=[pl.BlockSpec(memory_space=pl.ANY)] * 2,
        scratch_shapes=[dma((2,)), dma((rows,)), dma((rows,)), dma((cols,)), dma((cols,))]
        + [dma((cols,))] * 4
        + [dma((chips,))] * 4,
        compiler_params=pltpu.CompilerParams(collective_id=0, has_side_effects=True),
        name="exchange",
    )(white)
    row_all = row_all.reshape(windows, double_bins, width)
    col_all = col_all.reshape(windows, per, double_bins, width)

    depth = 2 * BINS
    return pl.pallas_call(
        functools.partial(pairs_kernel, float(windows) ** (-0.5)),
        grid=(bands,),
        out_shape=jax.ShapeDtypeStruct((2, half, width, per * width), jnp.bfloat16),
        in_specs=[
            pl.BlockSpec((windows, depth, width), lambda b: (0, b, 0)),
            pl.BlockSpec((windows, per, depth, width), lambda b: (0, 0, b, 0)),
        ],
        out_specs=pl.BlockSpec((2, BINS, width, per * width), lambda b: (0, b, 0, 0)),
        scratch_shapes=[pltpu.VMEM((1 + per, windows * depth, 128), jnp.float32)],
        compiler_params=pltpu.CompilerParams(vmem_limit_bytes=48 * 1024 * 1024),
        name="pairs",
    )(row_all, col_all)


def solution(mesh):
    placed = (P(("row", "col"), None, None), P(("row", "col"), None), P(), P())
    return jax.shard_map(
        functools.partial(body, mesh.shape["row"], mesh.shape["col"]),
        mesh=mesh, in_specs=placed, out_specs=P(None, None, "row", "col"), check_vma=False,
    )
```

time: 317 us -> 115 us (0.36); the launches traced: 312 us -> 114 us
  Pallas kernels: 0 us -> 107 us
  matrix products: 68.9 us -> 0 us
  other arithmetic: 68.1 us -> 3.75 us
  blocking collectives: 62.8 us -> 0 us
  waiting for transfers between devices: 60.5 us -> 0 us
  local copies, waits for them, and re-layouts: 37.4 us -> 4.01 us
  between operations: 13.9 us -> 0.06 us
    pallas_call x0 -> x3, Pallas kernels: none -> 107 us  [the longest x1 68.3 us: body(): pl.pallas_call(functools.partial(exchange_kernel, rows, cols), out_shape=...]
    dot_general x5 -> x0, matrix products: 68.9 us -> none  [the longest x4 56.6 us: pair_product(): jnp.einsum('wfa,wfb->fab', left, right, preferred_element_type=jnp.float32)]
    all_to_all x2 -> x0, blocking collectives: 62.8 us -> none  [the longest x1 38.7 us: body(): lax.all_to_all(col_source, ('row', 'col'), split_axis=2, concat_axis=0, t...]
    all_gather x2 -> x0, waiting for transfers between devices: 60.5 us -> none  [the longest x1 41.5 us: body(): col_block = lax.all_gather(col_local, 'row', axis=2, tiled=True)]
    convert_element_type x2 -> x0, other arithmetic: 23.7 us -> none  [the longest x1 23 us: body(): return (stacked * scaling).astype(jnp.bfloat16)]
    cos x1 -> x0, other arithmetic: 23.5 us -> none  [make_table(): jnp.cos(angles)]
    all_gather x2 -> x0, local copies, waits for them, and re-layouts: 13.9 us -> none  [the longest x1 9.43 us: body(): col_block = lax.all_gather(col_local, 'row', axis=2, tiled=True)]
    gather x3 -> x0, local copies, waits for them, and re-layouts: 13.1 us -> none  [the longest x2 8.62 us: body(): col_source = jnp.take(whitened, jnp.take(station_map, col_order), axis=2)]
  transfers between devices with their start and end apart: 2 -> 0, of which waited for: 2 -> 0; matrix products, arithmetic and copies ran while one was open for 8% -> 0% of each run, Pallas kernels for 0% -> 0%
where the time goes in v1:
time: 115 us; the launch traced here: 114 us
  Pallas kernels  107 us (93%)
  local copies, waits for them, and re-layouts  4.01 us (3%)
  other arithmetic  3.75 us (3%)
    pallas_call x1, Pallas kernels, body(): pl.pallas_call(functools.partial(exchange_kernel, rows, cols), out_shape=...  68.3 us
    pallas_call x1, Pallas kernels, body(): pl.pallas_call(functools.partial(spectra_kernel, length), grid=(steps,),...  19.8 us
    pallas_call x1, Pallas kernels, body(): pl.pallas_call(functools.partial(pairs_kernel, float(windows) ** (-0.5)),...  18.4 us
    unnamed x8, local copies, waits for them, and re-layouts  3.93 us
    sin x1, other arithmetic, parts(): return (jnp.cos(angles), jnp.sin(angles))  2.61 us

profile of v1, /device:TPU:0, one launch (start us, length us, event | category | flops | bytes accessed | tf_op | source)
XLA Modules:
  0.0 114.4 jit_solution(13970393446340359664)
XLA Ops:
  0.0 0.7 iota_add_fusion
  0.7 0.1 add.35
  0.8 0.4 sine_multiply_fusion
  1.2 2.6 %fusion.6 = (f32[160,1024]{1,0:T(8,128)S(1)}, f32[160,1024]{1,0:T(8,128)S(1)}) fusion(s32[160]{0:T(256)S(1)} %add.35), kind=kLoop, calls=%fused_computation.9 | loop fusion | flops 2293760 | bytes 1311360 | tf_op jit(solution)/shard_map/sin | solution.py:22
  3.8 0.0 copy-start.2
  3.9 0.7 copy-done.2
  4.5 0.0 copy-start.3
  4.5 0.7 copy-done.3
  5.2 19.8 %spectra.1.white = bf16[8,320,128]{2,1,0:T(8,128)(2,1)S(1)} custom-call(bf16[1,1024,8192]{2,1,0:T(8,128)(2,1)} %wave.1, f32[160,1024]{1,0:T(8,128)S(1)} %get-tuple-element.12.fine_cos, f32[160,1024]{1,0:T(8,128)S(1)} %get-tuple-element.11.fine_sin, f32[160,128]{1,0:T(8,128)S(1)} %get-tuple-element.10.coarse_cos, f32[160,128]{1,0:T(8,128)S(1)} %get-tuple-element.9.coarse_sin, ...), custom_call_target="tpu_custom_call" | custom-call | tf_op jit(solution)/shard_map/spectra/pallas_call | solution.py:297
  25.1 0.0 copy-start
  25.1 0.8 copy-done
  25.9 68.3 %exchange.1 = (bf16[4,8,320,128]{3,2,1,0:T(8,128)(2,1)}, bf16[4,8,2,320,128]{4,3,2,1,0:T(8,128)(2,1)}) custom-call(bf16[8,320,128]{2,1,0:T(8,128)(2,1)} %copy-done), custom_call_target="tpu_custom_call" | custom-call | tf_op jit(solution)/shard_map/exchange/pallas_call | solution.py:322
  94.2 0.0 copy-start.1
  94.2 1.7 %copy-done.1 = bf16[4,8,320,128]{3,2,1,0:T(8,128)(2,1)S(1)} copy-done((bf16[4,8,320,128]{3,2,1,0:T(8,128)(2,1)S(1)}, bf16[4,8,320,128]{3,2,1,0:T(8,128)(2,1)}, u32[]{:S(2)}) %copy-start.1) | copy-done | bytes 2621464
  96.0 18.4 %pairs.1 = bf16[2,160,128,256]{3,2,1,0:T(8,128)(2,1)} custom-call(bf16[32,320,128]{2,1,0:T(8,128)(2,1)S(1)} %bitcast.3, bf16[32,2,320,128]{3,2,1,0:T(8,128)(2,1)} %bitcast.5), custom_call_target="tpu_custom_call" | custom-call | tf_op jit(solution)/shard_map/pairs/pallas_call | solution.py:340
  (1 shorter events, 0.0 us)
Async XLA Ops:
  3.8 0.7 copy-start.2
  4.5 0.7 copy-start.3
  25.1 0.8 copy-start
  94.2 1.7 %copy-start.1 = (bf16[4,8,320,128]{3,2,1,0:T(8,128)(2,1)S(1)}, bf16[4,8,320,128]{3,2,1,0:T(8,128)(2,1)}, u32[]{:S(2)}) copy-start(bf16[4,8,320,128]{3,2,1,0:T(8,128)(2,1)} %get-tuple-element.7) | copy-start | bytes 7864324

commit v2 on v1

--- a/solution.py
+++ b/solution.py
@@ -10,25 +10,22 @@
 
 BINS = 16
 CHUNK = 1024
+PIECES = 2
+VMEM_BYTES = 60 * 1024 * 1024
 MESH = pl.DeviceIdType.MESH
 
 
 def phase_tables(band_starts, length):
     frequency = (band_starts[:, None] + jnp.arange(BINS, dtype=jnp.int32)[None, :]).reshape(-1)
-
-    def parts(samples):
-        phase = frequency[:, None] * samples[None, :] % length
-        angles = phase.astype(jnp.float32) * jnp.float32(2.0 * math.pi / length)
-        return jnp.cos(angles), jnp.sin(angles)
-
-    fine = parts(jnp.arange(CHUNK, dtype=jnp.int32))
-    coarse = parts(jnp.arange(128, dtype=jnp.int32) * CHUNK)
-    scaling = jnp.float32(length ** (-0.5))
-    return fine + (coarse[0] * scaling, coarse[1] * scaling)
+    samples = jnp.arange(128, dtype=jnp.int32)
+    samples = jnp.stack([samples, samples * 128])
+    phase = frequency[None, :, None] * samples[:, None, :] % length
+    angles = phase.astype(jnp.float32) * jnp.float32(2.0 * math.pi / length)
+    return jnp.cos(angles), jnp.sin(angles)
 
 
 def spectra_kernel(
-    length, wave, fine_cos, fine_sin, coarse_cos, coarse_sin, mask, order, out, acc, squares, white
+    length, wave, cosines, sines, mask, order, out, acc, squares, white, fine_cos, fine_sin
 ):
     step = pl.program_id(0)
     stations = wave.shape[1]
@@ -39,10 +36,17 @@
     def _():
         acc[...] = jnp.zeros_like(acc)
         squares[...] = jnp.zeros_like(squares)
-
-    lane = lax.broadcasted_iota(jnp.int32, coarse_cos.shape, 1)
-    first_cos = jnp.sum(jnp.where(lane == step, coarse_cos[...], 0.0), axis=1, keepdims=True)
-    first_sin = jnp.sum(jnp.where(lane == step, coarse_sin[...], 0.0), axis=1, keepdims=True)
+        for tile in range(CHUNK // 128):
+            tile_cos = cosines[1, :, tile : tile + 1]
+            tile_sin = sines[1, :, tile : tile + 1]
+            lanes = slice(tile * 128, (tile + 1) * 128)
+            fine_cos[:, lanes] = tile_cos * cosines[0] - tile_sin * sines[0]
+            fine_sin[:, lanes] = tile_sin * cosines[0] + tile_cos * sines[0]
+
+    scale = length ** (-0.5)
+    here = lax.broadcasted_iota(jnp.int32, cosines.shape[1:], 1) == step * (CHUNK // 128)
+    first_cos = scale * jnp.sum(jnp.where(here, cosines[1], 0.0), axis=1, keepdims=True)
+    first_sin = scale * jnp.sum(jnp.where(here, sines[1], 0.0), axis=1, keepdims=True)
     real = (first_cos * fine_cos[...] - first_sin * fine_sin[...]).astype(jnp.bfloat16)
     imag = (-(first_sin * fine_cos[...]) - first_cos * fine_sin[...]).astype(jnp.bfloat16)
     table = jnp.concatenate(
@@ -51,11 +55,12 @@
     acc[...] += lax.dot_general(
         table, wave[0], (((1,), (1,)), ((), ())), preferred_element_type=jnp.float32
     )
-    total = squares[...]
-    for tile in range(CHUNK // 128):
-        part = wave[0, :, tile * 128 : (tile + 1) * 128].astype(jnp.float32)
-        total = total + part * part
-    squares[...] = total
+    for top in range(0, stations, 64):
+        total = squares[top : top + 64, :]
+        for tile in range(CHUNK // 128):
+            part = wave[0, top : top + 64, tile * 128 : (tile + 1) * 128].astype(jnp.float32)
+            total = total + part * part
+        squares[top : top + 64, :] = total
 
     @pl.when(step == pl.num_programs(0) - 1)
     def _():
@@ -149,53 +154,33 @@
         ).wait_recv()
     own_row.wait()
 
-    def to_right(step):
-        block = c - step
-        return remote(
-            row_all.at[block], row_all.at[block],
-            right_sent.at[step], right_got.at[step], (r, c + 1),
-        )
-
-    def to_left(step):
-        block = c + step
-        return remote(
-            row_all.at[block], row_all.at[block],
-            left_sent.at[step], left_got.at[step], (r, c - 1),
-        )
-
-    def from_left(step):
-        block = c - 1 - step
-        return remote(
-            row_all.at[block], row_all.at[block],
-            right_sent.at[step], right_got.at[step], (r, c - 1),
-        )
-
-    def from_right(step):
-        block = c + 1 + step
-        return remote(
-            row_all.at[block], row_all.at[block],
-            left_sent.at[step], left_got.at[step], (r, c + 1),
-        )
-
-    def sends(step, act):
+    def piece_of(block, piece):
+        return row_all.at[block, pl.ds(piece * (rows // PIECES), rows // PIECES)]
+
+    def passing(block, piece, sent, got, step, target):
+        ref = piece_of(block, piece)
+        return remote(ref, ref, sent.at[step, piece], got.at[step, piece], (r, target))
+
+    def sends(step, piece, act):
         @pl.when((c + 1 < cols) & (c - step >= 0))
         def _():
-            act(to_right(step))
+            act(passing(c - step, piece, right_sent, right_got, step, c + 1))
 
         @pl.when((c - 1 >= 0) & (c + step < cols))
         def _():
-            act(to_left(step))
-
-    def receives(step):
+            act(passing(c + step, piece, left_sent, left_got, step, c - 1))
+
+    def receives(step, piece):
         @pl.when(c - 1 - step >= 0)
         def _():
-            from_left(step).wait_recv()
+            passing(c - 1 - step, piece, right_sent, right_got, step, c - 1).wait_recv()
 
         @pl.when(c + 1 + step < cols)
         def _():
-            from_right(step).wait_recv()
-
-    sends(0, lambda copy: copy.start())
+            passing(c + 1 + step, piece, left_sent, left_got, step, c + 1).wait_recv()
+
+    for piece in range(PIECES):
+        sends(0, piece, lambda copy: copy.start())
 
     for d in range(1, cols):
         other = lax.rem(c + cols - d, cols)
@@ -235,52 +220,66 @@
         to_chip(d).start()
     to_twin(0).start()
 
-    for step in range(max(cols - 1, chips - 1)):
-        if step < cols - 1:
-            receives(step)
-            if step + 1 < cols - 1:
-                sends(step + 1, lambda copy: copy.start())
-        if step + 1 < chips:
-            from_chip(step + 1).wait_recv()
-            to_twin(step + 1).start()
+    for step in range(cols - 2):
+        for piece in range(PIECES):
+            receives(step, piece)
+            sends(step + 1, piece, lambda copy: copy.start())
+    for d in range(1, chips):
+        from_chip(d).wait_recv()
+        to_twin(d).start()
+    for piece in range(PIECES):
+        receives(cols - 2, piece)
     for d in range(chips):
         from_twin(d).wait_recv()
     for copy in col_first + row_first:
         copy.wait_send()
     for step in range(cols - 1):
-        sends(step, lambda copy: copy.wait_send())
+        for piece in range(PIECES):
+            sends(step, piece, lambda copy: copy.wait_send())
     for d in range(1, chips):
         to_chip(d).wait_send()
     for d in range(chips):
         to_twin(d).wait_send()
 
 
-def pairs_kernel(scaling, row_block, col_block, out, spread):
-    windows, depth, width = row_block.shape
+def pairs_kernel(scaling, row_block, col_block, out):
+    windows, _, width = row_block.shape
     per = col_block.shape[1]
-    for window in range(windows):
-        lines = pl.ds(window * depth, depth)
-        spread[0, lines, 0:width] = row_block[window].astype(jnp.float32)
-        for part in range(per):
-            spread[1 + part, lines, 0:width] = col_block[window, part].astype(jnp.float32)
-
-    def pick(plane, line):
-        picked = spread[plane, pl.ds(line, windows, stride=depth), :]
-        return picked[:, 0:width].astype(jnp.bfloat16)
-
+    group = 16
+    side = group * BINS
+    into = lax.broadcasted_iota(jnp.int32, (side, side), 0)
+    source = lax.broadcasted_iota(jnp.int32, (side, side), 1)
+    swap = (into % group == source // BINS) & (into // group == source % BINS)
+    swap = swap.astype(jnp.float32).astype(jnp.bfloat16)
+
+    regrouped = []
+    for part in range(2):
+        bins = slice(part * BINS, (part + 1) * BINS)
+        for first in range(0, windows, group):
+            pieces = [row_block[first : first + group, bins, :].reshape(side, width)]
+            for block in range(per):
+                pieces.append(col_block[first : first + group, block, bins, :].reshape(side, width))
+            regrouped.append(
+                jnp.dot(
+                    swap, jnp.concatenate(pieces, axis=1), preferred_element_type=jnp.float32
+                ).astype(jnp.bfloat16)
+            )
+    half = len(regrouped) // 2
+    wide = per * width
     for bin_ in range(BINS):
-        left = jnp.concatenate([pick(0, bin_), pick(0, BINS + bin_)], axis=0)
-        real = jnp.concatenate([pick(1 + part, bin_) for part in range(per)], axis=1)
-        imag = jnp.concatenate([pick(1 + part, BINS + bin_) for part in range(per)], axis=1)
-        right = jnp.concatenate(
-            [jnp.concatenate([real, imag], axis=0), jnp.concatenate([imag, -real], axis=0)], axis=1
-        )
-        both = lax.dot_general(
-            left, right, (((0,), (0,)), ((), ())), preferred_element_type=jnp.float32
+        lines = slice(bin_ * group, (bin_ + 1) * group)
+        both = jnp.concatenate([block[lines] for block in regrouped], axis=0)
+        swapped = jnp.concatenate(
+            [block[lines, width:] for block in regrouped[half:]]
+            + [-block[lines, width:] for block in regrouped[:half]],
+            axis=0,
+        )
+        right = jnp.concatenate([both[:, width:], swapped], axis=1)
+        result = lax.dot_general(
+            both[:, 0:width], right, (((0,), (0,)), ((), ())), preferred_element_type=jnp.float32
         ) * scaling
-        wide = per * width
-        out[0, bin_] = both[:, 0:wide].astype(jnp.bfloat16)
-        out[1, bin_] = both[:, wide : 2 * wide].astype(jnp.bfloat16)
+        out[0, bin_] = result[:, 0:wide].astype(jnp.bfloat16)
+        out[1, bin_] = result[:, wide : 2 * wide].astype(jnp.bfloat16)
 
 
 def body(rows, cols, waveform, valid_mask, band_starts, station_map):
@@ -300,10 +299,8 @@
         out_shape=jax.ShapeDtypeStruct((rows, double_bins, width), jnp.bfloat16),
         in_specs=[
             pl.BlockSpec((1, stations, CHUNK), lambda i: (0, 0, i)),
-            whole((half, CHUNK)),
-            whole((half, CHUNK)),
-            whole((half, 128)),
-            whole((half, 128)),
+            whole((2, half, 128)),
+            whole((2, half, 128)),
             whole((1, stations)),
             whole((1, stations)),
         ],
@@ -312,8 +309,10 @@
             pltpu.VMEM((double_bins, stations), jnp.float32),
             pltpu.VMEM((stations, 128), jnp.float32),
             pltpu.VMEM((double_bins, stations), jnp.bfloat16),
+            pltpu.VMEM((half, CHUNK), jnp.float32),
+            pltpu.VMEM((half, CHUNK), jnp.float32),
         ],
-        compiler_params=pltpu.CompilerParams(vmem_limit_bytes=48 * 1024 * 1024),
+        compiler_params=pltpu.CompilerParams(vmem_limit_bytes=VMEM_BYTES),
         name="spectra",
     )(waveform, *tables, valid_mask, station_map[None, :])
 
@@ -328,9 +327,10 @@
         in_specs=[pl.BlockSpec(memory_space=pl.ANY)],
         out_specs=[pl.BlockSpec(memory_space=pl.ANY)] * 2,
         scratch_shapes=[dma((2,)), dma((rows,)), dma((rows,)), dma((cols,)), dma((cols,))]
-        + [dma((cols,))] * 4
+        + [dma((cols, PIECES))] * 4
         + [dma((chips,))] * 4,
-        compiler_params=pltpu.CompilerParams(collective_id=0, has_side_effects=True),
+        compiler_params=pltpu.CompilerParams(collective_id=0, has_side_effects=True, vmem_limit_bytes=VMEM_BYTES
+        ),
         name="exchange",
     )(white)
     row_all = row_all.reshape(windows, double_bins, width)
@@ -346,8 +346,7 @@
             pl.BlockSpec((windows, per, depth, width), lambda b: (0, 0, b, 0)),
         ],
         out_specs=pl.BlockSpec((2, BINS, width, per * width), lambda b: (0, b, 0, 0)),
-        scratch_shapes=[pltpu.VMEM((1 + per, windows * depth, 128), jnp.float32)],
-        compiler_params=pltpu.CompilerParams(vmem_limit_bytes=48 * 1024 * 1024),
+        compiler_params=pltpu.CompilerParams(vmem_limit_bytes=VMEM_BYTES),
         name="pairs",
     )(row_all, col_all)
 

time: 115 us -> 96.3 us (0.84)
  Pallas kernels: 107 us -> 93.4 us
  local copies, waits for them, and re-layouts: 4.01 us -> 0.08 us
  other arithmetic: 3.75 us -> 2.19 us
    pallas_call x1, Pallas kernels: 68.3 us -> 60.9 us  [body(): pl.pallas_call(functools.partial(exchange_kernel, rows, cols), out_shape=...]
    unnamed x8 -> x0, local copies, waits for them, and re-layouts: 3.93 us -> none
    pallas_call x1, Pallas kernels: 19.8 us -> 16.1 us  [body(): pl.pallas_call(functools.partial(spectra_kernel, length), grid=(steps,),...]
    pallas_call x1, Pallas kernels: 18.4 us -> 16.4 us  [body(): pl.pallas_call(functools.partial(pairs_kernel, float(windows) ** (-0.5)),...]
    sin x1, other arithmetic: 2.61 us -> 1.45 us  [phase_tables(): return (jnp.cos(angles), jnp.sin(angles))]
where the time goes in v2:
time: 96.3 us; the launch traced here: 95.7 us
  Pallas kernels  93.4 us (97%)
  other arithmetic  2.19 us (2%)
    pallas_call x1, Pallas kernels, body(): pl.pallas_call(functools.partial(exchange_kernel, rows, cols), out_shape=...  60.9 us
    pallas_call x1, Pallas kernels, body(): pl.pallas_call(functools.partial(pairs_kernel, float(windows) ** (-0.5)),...  16.4 us
    pallas_call x1, Pallas kernels, body(): pl.pallas_call(functools.partial(spectra_kernel, length), grid=(steps,),...  16.1 us

profile of v2, /device:TPU:0, one launch (start us, length us, event | category | flops | bytes accessed | tf_op | source)
XLA Modules:
  0.0 95.7 jit_solution(10156830997581100805)
XLA Ops:
  0.0 0.7 iota_add_fusion
  0.7 0.1 add.29
  0.8 1.4 %fusion.3 = (f32[2,160,128]{2,1,0:T(8,128)}, f32[2,160,128]{2,1,0:T(8,128)}) fusion(s32[2,128]{1,0:T(2,128)S(1)} %pad_add_fusion, s32[160]{0:T(256)S(1)} %add.29), kind=kLoop, calls=%fused_computation.8 | loop fusion | flops 573440 | bytes 329344 | tf_op jit(solution)/shard_map/sin | solution.py:24
  2.3 16.1 %spectra.1.white = bf16[8,320,128]{2,1,0:T(8,128)(2,1)} custom-call(bf16[1,1024,8192]{2,1,0:T(8,128)(2,1)} %wave.1, f32[2,160,128]{2,1,0:T(8,128)} %get-tuple-element.10.cosines, f32[2,160,128]{2,1,0:T(8,128)} %get-tuple-element.9.sines, s32[1,1024]{1,0:T(1,128)} %mask.1, s32[1,1024]{1,0:T(1,128)} %bitcast.5), custom_call_target="tpu_custom_call" | custom-call | tf_op jit(solution)/shard_map/spectra/pallas_call | solution.py:296
  18.4 60.9 %exchange.1 = (bf16[4,8,320,128]{3,2,1,0:T(8,128)(2,1)}, bf16[4,8,2,320,128]{4,3,2,1,0:T(8,128)(2,1)}) custom-call(bf16[8,320,128]{2,1,0:T(8,128)(2,1)} %spectra.1.white), custom_call_target="tpu_custom_call" | custom-call | tf_op jit(solution)/shard_map/exchange/pallas_call | solution.py:321
  79.3 16.4 %pairs.1 = bf16[2,160,128,256]{3,2,1,0:T(8,128)(2,1)} custom-call(bf16[32,320,128]{2,1,0:T(8,128)(2,1)} %bitcast.4, bf16[32,2,320,128]{3,2,1,0:T(8,128)(2,1)} %bitcast.3), custom_call_target="tpu_custom_call" | custom-call | tf_op jit(solution)/shard_map/pairs/pallas_call | solution.py:340
  (3 shorter events, 0.0 us)

commit v3 on v2

--- a/solution.py
+++ b/solution.py
@@ -266,20 +266,28 @@
             )
     half = len(regrouped) // 2
     wide = per * width
-    for bin_ in range(BINS):
-        lines = slice(bin_ * group, (bin_ + 1) * group)
-        both = jnp.concatenate([block[lines] for block in regrouped], axis=0)
-        swapped = jnp.concatenate(
-            [block[lines, width:] for block in regrouped[half:]]
-            + [-block[lines, width:] for block in regrouped[:half]],
-            axis=0,
-        )
-        right = jnp.concatenate([both[:, width:], swapped], axis=1)
-        result = lax.dot_general(
-            both[:, 0:width], right, (((0,), (0,)), ((), ())), preferred_element_type=jnp.float32
-        ) * scaling
-        out[0, bin_] = result[:, 0:wide].astype(jnp.bfloat16)
-        out[1, bin_] = result[:, wide : 2 * wide].astype(jnp.bfloat16)
+    together = max(1, 256 // (2 * windows))
+    depth = together * 2 * windows
+    owner = lax.broadcasted_iota(jnp.int32, (width, depth), 1) // (2 * windows)
+    masks = [(owner == j).astype(jnp.float32).astype(jnp.bfloat16) for j in range(together)]
+    for first in range(0, BINS, together):
+        both, turned = [], []
+        for bin_ in range(first, first + together):
+            lines = slice(bin_ * group, (bin_ + 1) * group)
+            both += [block[lines] for block in regrouped]
+            turned += [-block[lines, 0:width] for block in regrouped[half:]]
+            turned += [block[lines, 0:width] for block in regrouped[:half]]
+        both = jnp.concatenate(both, axis=0)
+        sides = [both[:, 0:width].T, jnp.concatenate(turned, axis=0).T]
+        if together > 1:
+            sides = [side * mask for mask in masks for side in sides]
+        result = jnp.dot(
+            jnp.concatenate(sides, axis=0), both[:, width:], preferred_element_type=jnp.float32
+        )
+        for j in range(together):
+            for part in range(2):
+                top = (2 * j + part) * width
+                out[part, first + j] = (result[top : top + width] * scaling).astype(jnp.bfloat16)
 
 
 def body(rows, cols, waveform, valid_mask, band_starts, station_map):

time: 96.3 us -> 96.3 us (level)
  no operation moved by 1% of the time
where the time goes in v3:
time: 96.3 us; the launch traced here: 95.7 us
  Pallas kernels  93.4 us (97%)
  other arithmetic  2.19 us (2%)
    pallas_call x1, Pallas kernels, body(): pl.pallas_call(functools.partial(exchange_kernel, rows, cols), out_shape=...  60.9 us
    pallas_call x1, Pallas kernels, body(): pl.pallas_call(functools.partial(pairs_kernel, float(windows) ** (-0.5)),...  16.4 us
    pallas_call x1, Pallas kernels, body(): pl.pallas_call(functools.partial(spectra_kernel, length), grid=(steps,),...  16.1 us

profile of v3, /device:TPU:0, one launch (start us, length us, event | category | flops | bytes accessed | tf_op | source)
XLA Modules:
  0.0 95.7 jit_solution(721759613109922401)
XLA Ops:
  0.0 0.7 iota_add_fusion
  0.7 0.1 add.29
  0.8 1.4 %fusion.3 = (f32[2,160,128]{2,1,0:T(8,128)}, f32[2,160,128]{2,1,0:T(8,128)}) fusion(s32[2,128]{1,0:T(2,128)S(1)} %pad_add_fusion, s32[160]{0:T(256)S(1)} %add.29), kind=kLoop, calls=%fused_computation.8 | loop fusion | flops 573440 | bytes 329344 | tf_op jit(solution)/shard_map/sin | solution.py:24
  2.3 16.1 %spectra.1.white = bf16[8,320,128]{2,1,0:T(8,128)(2,1)} custom-call(bf16[1,1024,8192]{2,1,0:T(8,128)(2,1)} %wave.1, f32[2,160,128]{2,1,0:T(8,128)} %get-tuple-element.10.cosines, f32[2,160,128]{2,1,0:T(8,128)} %get-tuple-element.9.sines, s32[1,1024]{1,0:T(1,128)} %mask.1, s32[1,1024]{1,0:T(1,128)} %bitcast.5), custom_call_target="tpu_custom_call" | custom-call | tf_op jit(solution)/shard_map/spectra/pallas_call | solution.py:304
  18.4 60.9 %exchange.1 = (bf16[4,8,320,128]{3,2,1,0:T(8,128)(2,1)}, bf16[4,8,2,320,128]{4,3,2,1,0:T(8,128)(2,1)}) custom-call(bf16[8,320,128]{2,1,0:T(8,128)(2,1)} %spectra.1.white), custom_call_target="tpu_custom_call" | custom-call | tf_op jit(solution)/shard_map/exchange/pallas_call | solution.py:329
  79.3 16.4 %pairs.1 = bf16[2,160,128,256]{3,2,1,0:T(8,128)(2,1)} custom-call(bf16[32,320,128]{2,1,0:T(8,128)(2,1)} %bitcast.4, bf16[32,2,320,128]{3,2,1,0:T(8,128)(2,1)} %bitcast.3), custom_call_target="tpu_custom_call" | custom-call | tf_op jit(solution)/shard_map/pairs/pallas_call | solution.py:348
  (3 shorter events, 0.0 us)

commit v4 on v3

--- a/solution.py
+++ b/solution.py
@@ -11,6 +11,7 @@
 BINS = 16
 CHUNK = 1024
 PIECES = 2
+VIEWS = 4
 VMEM_BYTES = 60 * 1024 * 1024
 MESH = pl.DeviceIdType.MESH
 
@@ -25,10 +26,13 @@
 
 
 def spectra_kernel(
-    length, wave, cosines, sines, mask, order, out, acc, squares, white, fine_cos, fine_sin
+    length, *refs
 ):
+    waves, refs = refs[:VIEWS], refs[VIEWS:]
+    cosines, sines, mask, order, out, acc, squares, white, fine_cos, fine_sin = refs
     step = pl.program_id(0)
-    stations = wave.shape[1]
+    each = waves[0].shape[1]
+    stations = each * VIEWS
     double_bins = acc.shape[0]
     bands = double_bins // (2 * BINS)
 
@@ -52,15 +56,17 @@
     table = jnp.concatenate(
         [real.reshape(bands, BINS, CHUNK), imag.reshape(bands, BINS, CHUNK)], axis=1
     ).reshape(double_bins, CHUNK)
-    acc[...] += lax.dot_general(
-        table, wave[0], (((1,), (1,)), ((), ())), preferred_element_type=jnp.float32
-    )
-    for top in range(0, stations, 64):
-        total = squares[top : top + 64, :]
-        for tile in range(CHUNK // 128):
-            part = wave[0, top : top + 64, tile * 128 : (tile + 1) * 128].astype(jnp.float32)
-            total = total + part * part
-        squares[top : top + 64, :] = total
+    for view, wave in enumerate(waves):
+        base = view * each
+        acc[:, base : base + each] += lax.dot_general(
+            table, wave[0], (((1,), (1,)), ((), ())), preferred_element_type=jnp.float32
+        )
+        for top in range(0, each, 64):
+            total = squares[base + top : base + top + 64, :]
+            for tile in range(CHUNK // 128):
+                part = wave[0, top : top + 64, tile * 128 : (tile + 1) * 128].astype(jnp.float32)
+                total = total + part * part
+            squares[base + top : base + top + 64, :] = total
 
     @pl.when(step == pl.num_programs(0) - 1)
     def _():
@@ -242,7 +248,10 @@
         to_twin(d).wait_send()
 
 
-def pairs_kernel(scaling, row_block, col_block, out):
+def pairs_kernel(scaling, row_block, col_block, out, held, sems):
+    step = pl.program_id(0)
+    last = pl.num_programs(0) - 1
+    slot = lax.rem(step, 2)
     windows, _, width = row_block.shape
     per = col_block.shape[1]
     group = 16
@@ -269,6 +278,25 @@
     together = max(1, 256 // (2 * windows))
     depth = together * 2 * windows
     owner = lax.broadcasted_iota(jnp.int32, (width, depth), 1) // (2 * windows)
+    groups = BINS // together
+
+    def copies(at_step, at_slot):
+        return [
+            pltpu.make_async_copy(
+                held.at[at_slot, part, pl.ds(g * together, together)],
+                out.at[part, pl.ds(at_step * BINS + g * together, together)],
+                sems.at[at_slot, part, g],
+            )
+            for g in range(groups)
+            for part in range(2)
+        ]
+
+    @pl.when(step >= 2)
+    def _():
+        for copy in copies(step - 2, slot):
+            copy.wait()
+
+    outgoing = copies(step, slot)
     masks = [(owner == j).astype(jnp.float32).astype(jnp.bfloat16) for j in range(together)]
     for first in range(0, BINS, together):
         both, turned = [], []
@@ -287,7 +315,16 @@
         for j in range(together):
             for part in range(2):
                 top = (2 * j + part) * width
-                out[part, first + j] = (result[top : top + width] * scaling).astype(jnp.bfloat16)
+                held[slot, part, first + j] = (result[top : top + width] * scaling).astype(
+                    jnp.bfloat16
+                )
+        for part in range(2):
+            outgoing[first // together * 2 + part].start()
+
+    @pl.when(step == last)
+    def _():
+        for copy in copies(step - 1, 1 - slot) + outgoing:
+            copy.wait()
 
 
 def body(rows, cols, waveform, valid_mask, band_starts, station_map):
@@ -306,7 +343,10 @@
         grid=(steps,),
         out_shape=jax.ShapeDtypeStruct((rows, double_bins, width), jnp.bfloat16),
         in_specs=[
-            pl.BlockSpec((1, stations, CHUNK), lambda i: (0, 0, i)),
+            pl.BlockSpec((1, stations // VIEWS, CHUNK), lambda i, view=view: (0, view, i))
+            for view in range(VIEWS)
+        ]
+        + [
             whole((2, half, 128)),
             whole((2, half, 128)),
             whole((1, stations)),
@@ -322,7 +362,7 @@
         ],
         compiler_params=pltpu.CompilerParams(vmem_limit_bytes=VMEM_BYTES),
         name="spectra",
-    )(waveform, *tables, valid_mask, station_map[None, :])
+    )(*[waveform] * VIEWS, *tables, valid_mask, station_map[None, :])
 
     dma = pltpu.SemaphoreType.DMA
     chips = rows // 2
@@ -353,7 +393,11 @@
             pl.BlockSpec((windows, depth, width), lambda b: (0, b, 0)),
             pl.BlockSpec((windows, per, depth, width), lambda b: (0, 0, b, 0)),
         ],
-        out_specs=pl.BlockSpec((2, BINS, width, per * width), lambda b: (0, b, 0, 0)),
+        out_specs=pl.BlockSpec(memory_space=pl.ANY),
+        scratch_shapes=[
+            pltpu.VMEM((2, 2, BINS, width, per * width), jnp.bfloat16),
+            pltpu.SemaphoreType.DMA((2, 2, BINS)),
+        ],
         compiler_params=pltpu.CompilerParams(vmem_limit_bytes=VMEM_BYTES),
         name="pairs",
     )(row_all, col_all)

time: 96.3 us -> 96.3 us (level)
  no operation moved by 1% of the time
where the time goes in v4:
time: 96.3 us; the launch traced here: 95.7 us
  Pallas kernels  93.4 us (97%)
  other arithmetic  2.19 us (2%)
    pallas_call x1, Pallas kernels, body(): pl.pallas_call(functools.partial(exchange_kernel, rows, cols), out_shape=...  60.9 us
    pallas_call x1, Pallas kernels, body(): pl.pallas_call(functools.partial(pairs_kernel, float(windows) ** (-0.5)),...  16.4 us
    pallas_call x1, Pallas kernels, body(): pl.pallas_call(functools.partial(spectra_kernel, length), grid=(steps,),...  16.1 us

profile of v4, /device:TPU:0, one launch (start us, length us, event | category | flops | bytes accessed | tf_op | source)
XLA Modules:
  0.0 95.7 jit_solution(9319372417386340812)
XLA Ops:
  0.0 0.7 iota_add_fusion
  0.7 0.1 add.29
  0.8 1.4 %fusion.3 = (f32[2,160,128]{2,1,0:T(8,128)}, f32[2,160,128]{2,1,0:T(8,128)}) fusion(s32[2,128]{1,0:T(2,128)S(1)} %pad_add_fusion, s32[160]{0:T(256)S(1)} %add.29), kind=kLoop, calls=%fused_computation.8 | loop fusion | flops 573440 | bytes 329344 | tf_op jit(solution)/shard_map/sin | solution.py:25
  2.3 16.1 %spectra.1.white = bf16[8,320,128]{2,1,0:T(8,128)(2,1)} custom-call(bf16[1,1024,8192]{2,1,0:T(8,128)(2,1)} %refs_3_.1, bf16[1,1024,8192]{2,1,0:T(8,128)(2,1)} %refs_3_.1, bf16[1,1024,8192]{2,1,0:T(8,128)(2,1)} %refs_3_.1, bf16[1,1024,8192]{2,1,0:T(8,128)(2,1)} %refs_3_.1, f32[2,160,128]{2,1,0:T(8,128)} %get-tuple-element.10.refs_4_, ...), custom_call_target="tpu_custom_call" | custom-call | tf_op jit(solution)/shard_map/spectra/pallas_call | solution.py:341
  18.4 60.9 %exchange.1 = (bf16[4,8,320,128]{3,2,1,0:T(8,128)(2,1)}, bf16[4,8,2,320,128]{4,3,2,1,0:T(8,128)(2,1)}) custom-call(bf16[8,320,128]{2,1,0:T(8,128)(2,1)} %spectra.1.white), custom_call_target="tpu_custom_call" | custom-call | tf_op jit(solution)/shard_map/exchange/pallas_call | solution.py:369
  79.3 16.4 %pairs.1 = bf16[2,160,128,256]{3,2,1,0:T(8,128)(2,1)} custom-call(bf16[32,320,128]{2,1,0:T(8,128)(2,1)} %bitcast.4, bf16[32,2,320,128]{3,2,1,0:T(8,128)(2,1)} %bitcast.3), custom_call_target="tpu_custom_call" | custom-call | tf_op jit(solution)/shard_map/pairs/pallas_call | solution.py:388
  (3 shorter events, 0.0 us)

commit v5 on v4

v5 whole, which is shorter than its diff:
```python
import functools
import math

import jax
import jax.numpy as jnp
from jax import lax
from jax.experimental import pallas as pl
from jax.experimental.pallas import tpu as pltpu
from jax.sharding import PartitionSpec as P

BINS = 16
CHUNK = 1024
VMEM_BYTES = 60 * 1024 * 1024
MESH = pl.DeviceIdType.MESH


def phase_tables(band_starts, length):
    frequency = (band_starts[:, None] + jnp.arange(BINS, dtype=jnp.int32)[None, :]).reshape(-1)
    samples = jnp.arange(128, dtype=jnp.int32)
    samples = jnp.stack([samples, samples * 128])
    phase = frequency[None, :, None] * samples[:, None, :] % length
    angles = phase.astype(jnp.float32) * jnp.float32(2.0 * math.pi / length)
    return jnp.cos(angles), jnp.sin(angles)


def fill_fine(bins, cosines, sines, fine_cos, fine_sin):
    for tile in range(CHUNK // 128):
        tile_cos = cosines[1, bins, tile : tile + 1]
        tile_sin = sines[1, bins, tile : tile + 1]
        lanes = slice(tile * 128, (tile + 1) * 128)
        fine_cos[:, lanes] = tile_cos * cosines[0, bins] - tile_sin * sines[0, bins]
        fine_sin[:, lanes] = tile_sin * cosines[0, bins] + tile_cos * sines[0, bins]


def table_of(step, bins, length, cosines, sines, fine_cos, fine_sin):
    scale = length ** (-0.5)
    count = bins.stop - bins.start
    here = lax.broadcasted_iota(jnp.int32, (count, 128), 1) == step * (CHUNK // 128)
    first_cos = scale * jnp.sum(jnp.where(here, cosines[1, bins], 0.0), axis=1, keepdims=True)
    first_sin = scale * jnp.sum(jnp.where(here, sines[1, bins], 0.0), axis=1, keepdims=True)
    real = (first_cos * fine_cos[...] - first_sin * fine_sin[...]).astype(jnp.bfloat16)
    imag = (-(first_sin * fine_cos[...]) - first_cos * fine_sin[...]).astype(jnp.bfloat16)
    return jnp.concatenate(
        [real.reshape(-1, BINS, CHUNK), imag.reshape(-1, BINS, CHUNK)], axis=1
    ).reshape(2 * count, CHUNK)


def transform(table, wave):
    return lax.dot_general(
        table, wave, (((1,), (1,)), ((), ())), preferred_element_type=jnp.float32
    )


def whiten_and_place(acc, inverse, mask, order, white, out):
    stations = acc.shape[1]
    valid = mask[...].astype(jnp.float32)
    for top in range(0, acc.shape[0], 2 * BINS):
        re = acc[top : top + BINS, :] * inverse
        im = acc[top + BINS : top + 2 * BINS, :] * inverse
        power = re * re + im * im
        mean = jnp.mean(power, axis=0, keepdims=True)
        factor = valid / jnp.sqrt(power + mean + 0.1)
        white[top : top + BINS, :] = (re * factor).astype(jnp.bfloat16)
        white[top + BINS : top + 2 * BINS, :] = (im * factor).astype(jnp.bfloat16)
    width = out.shape[2]
    group = 256
    for start in range(0, stations, group):
        source = lax.broadcasted_iota(jnp.int32, (stations, group), 0)
        pick = (source == order[0:1, start : start + group]).astype(jnp.float32)
        placed = jnp.dot(
            white[...], pick.astype(jnp.bfloat16), preferred_element_type=jnp.float32
        ).astype(jnp.bfloat16)
        for inner in range(group // width):
            out[start // width + inner] = placed[:, inner * width : (inner + 1) * width]


def spectra_kernel(
    length, wave, cosines, sines, mask, order, out, inverse, acc, squares, white, fine_cos, fine_sin
):
    step = pl.program_id(0)
    stations = wave.shape[1]
    bins = slice(0, acc.shape[0] // 2)

    @pl.when(step == 0)
    def _():
        acc[...] = jnp.zeros_like(acc)
        squares[...] = jnp.zeros_like(squares)
        fill_fine(bins, cosines, sines, fine_cos, fine_sin)

    acc[...] += transform(
        table_of(step, bins, length, cosines, sines, fine_cos, fine_sin), wave[0]
    )
    for top in range(0, stations, 64):
        total = squares[top : top + 64, :]
        for tile in range(CHUNK // 128):
            part = wave[0, top : top + 64, tile * 128 : (tile + 1) * 128].astype(jnp.float32)
            total = total + part * part
        squares[top : top + 64, :] = total

    @pl.when(step == pl.num_programs(0) - 1)
    def _():
        ones = jnp.ones((8, 128), jnp.float32)
        sums = lax.dot_general(
            ones,
            squares[...],
            (((1,), (1,)), ((), ())),
            precision=lax.Precision.HIGHEST,
            preferred_element_type=jnp.float32,
        )[0:1]
        inverse[...] = 1.0 / jnp.sqrt(sums / length + 1e-06)
        whiten_and_place(acc, inverse[...], mask, order, white, out)


def exchange_kernel(
    rows, cols, ready, waveform, cosines, sines, mask, order, inverse, row_all, col_all,
    local_sem, row_sent, row_got, col_sent, col_got,
    right_sent, right_got, left_sent, left_got, chip_sent, chip_got, pair_sent, pair_got,
    waves, wave_sem, acc, white, fine_cos, fine_sin, later,
):
    r = lax.axis_index("row")
    c = lax.axis_index("col")
    chips = rows // 2
    core = lax.rem(r, 2)
    chip = r // 2
    twin = r + 1 - 2 * core
    per = rows // cols
    length = waveform.shape[2]
    steps = length // CHUNK
    sources = (ready, later)
    sizes = [source.shape[1] for source in sources]
    tops = (0, sizes[0])

    def fetch(step):
        slot = lax.rem(step, 2)
        return pltpu.make_async_copy(
            waveform.at[0, :, pl.ds(pl.multiple_of(step * CHUNK, CHUNK), CHUNK)],
            waves.at[slot],
            wave_sem.at[slot],
        )

    fetch(0).start()
    barrier = pltpu.get_barrier_semaphore()
    for d in range(1, rows):
        pl.semaphore_signal(
            barrier, inc=1, device_id=(lax.rem(r + d, rows), c), device_id_type=MESH
        )
    for d in range(1, cols):
        pl.semaphore_signal(
            barrier, inc=1, device_id=(r, lax.rem(c + d, cols)), device_id_type=MESH
        )
    pl.semaphore_wait(barrier, rows - 1 + cols - 1)

    def remote(src, dst, sent, got, target):
        return pltpu.make_async_remote_copy(
            src_ref=src, dst_ref=dst, send_sem=sent, recv_sem=got,
            device_id=target, device_id_type=MESH,
        )

    def lines(half):
        return pl.ds(tops[half], sizes[half])

    def col_part(half, block):
        return sources[half].at[pl.ds(block * per, per)]

    def col_first(half, d):
        other = lax.rem(c + d, cols)
        return remote(
            col_part(half, other), col_all.at[c, r, :, lines(half)],
            col_sent.at[half, d], col_got.at[half, d], (r, other),
        )

    def row_first(half, d):
        other = lax.rem(r + d, rows)
        return remote(
            sources[half].at[other], row_all.at[c, r, lines(half)],
            row_sent.at[half, d], row_got.at[half, d], (other, c),
        )

    def own_row(half):
        return pltpu.make_async_copy(
            sources[half].at[r], row_all.at[c, r, lines(half)], local_sem.at[half, 0]
        )

    def own_col(half):
        return pltpu.make_async_copy(
            col_part(half, c), col_all.at[c, r, :, lines(half)], local_sem.at[half, 1]
        )

    def start_firsts(half):
        for d in range(1, cols):
            col_first(half, d).start()
        for d in range(1, rows):
            row_first(half, d).start()
        own_row(half).start()
        own_col(half).start()

    def passing(block, half, sent, got, step, target):
        ref = row_all.at[block, :, lines(half)]
        return remote(ref, ref, sent.at[step, half], got.at[step, half], (r, target))

    def sends(step, half, act):
        @pl.when((c + 1 < cols) & (c - step >= 0))
        def _():
            act(passing(c - step, half, right_sent, right_got, step, c + 1))

        @pl.when((c - 1 >= 0) & (c + step < cols))
        def _():
            act(passing(c + step, half, left_sent, left_got, step, c - 1))

    def receives(step, half):
        @pl.when(c - 1 - step >= 0)
        def _():
            passing(c - 1 - step, half, right_sent, right_got, step, c - 1).wait_recv()

        @pl.when(c + 1 + step < cols)
        def _():
            passing(c + 1 + step, half, left_sent, left_got, step, c + 1).wait_recv()

    def moving(half, source, sent, got, d, target):
        ref = col_all.at[:, source, :, lines(half)]
        return remote(ref, ref, sent.at[half, d], got.at[half, d], (target, c))

    def to_chip(half, d):
        other = 2 * lax.rem(chip + d, chips) + core
        return moving(half, r, chip_sent, chip_got, d, other)

    def from_chip(half, d):
        other = 2 * lax.rem(chip + chips - d, chips) + core
        return moving(half, other, chip_sent, chip_got, d, other)

    def to_twin(half, d):
        source = 2 * lax.rem(chip + chips - d, chips) + core
        return moving(half, source, pair_sent, pair_got, d, twin)

    def from_twin(half, d):
        source = 2 * lax.rem(chip + chips - d, chips) + 1 - core
        return moving(half, source, pair_sent, pair_got, d, twin)

    def start_seconds(half):
        for d in range(1, rows):
            other = lax.rem(r + rows - d, rows)
            remote(
                sources[half].at[r], row_all.at[c, other, lines(half)],
                row_sent.at[half, d], row_got.at[half, d], (other, c),
            ).wait_recv()
        own_row(half).wait()
        sends(0, half, lambda copy: copy.start())
        for d in range(1, cols):
            other = lax.rem(c + cols - d, cols)
            remote(
                col_part(half, c), col_all.at[other, r, :, lines(half)],
                col_sent.at[half, d], col_got.at[half, d], (r, other),
            ).wait_recv()
        own_col(half).wait()
        for d in range(1, chips):
            to_chip(half, d).start()
        to_twin(half, 0).start()

    start_firsts(0)

    bins = slice(sizes[0] // 2, sum(sizes) // 2)
    acc[...] = jnp.zeros_like(acc)
    fill_fine(bins, cosines, sines, fine_cos, fine_sin)

    def chunk(step, carry):
        @pl.when(step + 1 < steps)
        def _():
            fetch(step + 1).start()

        fetch(step).wait()
        acc[...] += transform(
            table_of(step, bins, length, cosines, sines, fine_cos, fine_sin),
            waves[lax.rem(step, 2)],
        )
        return carry

    pause = max(1, steps * 3 // 4)
    lax.fori_loop(0, pause, chunk, 0)
    start_seconds(0)
    lax.fori_loop(pause, steps, chunk, 0)
    whiten_and_place(acc, inverse[...], mask, order, white, later)
    start_firsts(1)
    start_seconds(1)

    for step in range(cols - 2):
        for half in range(2):
            receives(step, half)
            sends(step + 1, half, lambda copy: copy.start())
    for half in range(2):
        for d in range(1, chips):
            from_chip(half, d).wait_recv()
            to_twin(half, d).start()
    for half in range(2):
        receives(cols - 2, half)
    for half in range(2):
        for d in range(chips):
            from_twin(half, d).wait_recv()
            to_twin(half, d).wait_send()
        for d in range(1, cols):
            col_first(half, d).wait_send()
        for d in range(1, rows):
            row_first(half, d).wait_send()
        for step in range(cols - 1):
            sends(step, half, lambda copy: copy.wait_send())
        for d in range(1, chips):
            to_chip(half, d).wait_send()


def pairs_kernel(scaling, row_block, col_block, out, held, sems):
    step = pl.program_id(0)
    last = pl.num_programs(0) - 1
    slot = lax.rem(step, 2)
    windows, _, width = row_block.shape
    per = col_block.shape[1]
    group = 16
    side = group * BINS
    into = lax.broadcasted_iota(jnp.int32, (side, side), 0)
    source = lax.broadcasted_iota(jnp.int32, (side, side), 1)
    swap = (into % group == source // BINS) & (into // group == source % BINS)
    swap = swap.astype(jnp.float32).astype(jnp.bfloat16)

    regrouped = []
    for part in range(2):
        bins = slice(part * BINS, (part + 1) * BINS)
        for first in range(0, windows, group):
            pieces = [row_block[first : first + group, bins, :].reshape(side, width)]
            for block in range(per):
                pieces.append(col_block[first : first + group, block, bins, :].reshape(side, width))
            regrouped.append(
                jnp.dot(
                    swap, jnp.concatenate(pieces, axis=1), preferred_element_type=jnp.float32
                ).astype(jnp.bfloat16)
            )
    half = len(regrouped) // 2
    wide = per * width
    together = max(1, 256 // (2 * windows))
    depth = together * 2 * windows
    owner = lax.broadcasted_iota(jnp.int32, (width, depth), 1) // (2 * windows)
    groups = BINS // together

    def copies(at_step, at_slot):
        return [
            pltpu.make_async_copy(
                held.at[at_slot, part, pl.ds(g * together, together)],
                out.at[part, pl.ds(at_step * BINS + g * together, together)],
                sems.at[at_slot, part, g],
            )
            for g in range(groups)
            for part in range(2)
        ]

    @pl.when(step >= 2)
    def _():
        for copy in copies(step - 2, slot):
            copy.wait()

    outgoing = copies(step, slot)
    masks = [(owner == j).astype(jnp.float32).astype(jnp.bfloat16) for j in range(together)]
    for first in range(0, BINS, together):
        both, turned = [], []
        for bin_ in range(first, first + together):
            lines = slice(bin_ * group, (bin_ + 1) * group)
            both += [block[lines] for block in regrouped]
            turned += [-block[lines, 0:width] for block in regrouped[half:]]
            turned += [block[lines, 0:width] for block in regrouped[:half]]
        both = jnp.concatenate(both, axis=0)
        sides = [both[:, 0:width].T, jnp.concatenate(turned, axis=0).T]
        if together > 1:
            sides = [side * mask for mask in masks for side in sides]
        result = jnp.dot(
            jnp.concatenate(sides, axis=0), both[:, width:], preferred_element_type=jnp.float32
        )
        for j in range(together):
            for part in range(2):
                top = (2 * j + part) * width
                held[slot, part, first + j] = (result[top : top + width] * scaling).astype(
                    jnp.bfloat16
                )
        for part in range(2):
            outgoing[first // together * 2 + part].start()

    @pl.when(step == last)
    def _():
        for copy in copies(step - 1, 1 - slot) + outgoing:
            copy.wait()


def body(rows, cols, waveform, valid_mask, band_starts, station_map):
    _, stations, length = waveform.shape
    bands = band_starts.shape[0]
    double_bins = 2 * BINS * bands
    half = double_bins // 2
    width = stations // rows
    per = rows // cols
    windows = rows * cols
    steps = length // CHUNK
    whole = lambda shape: pl.BlockSpec(shape, lambda i: (0,) * len(shape))
    tables = phase_tables(band_starts, length)
    order = station_map[None, :]
    sizes = (bands // 2 * 2 * BINS, (bands - bands // 2) * 2 * BINS)

    def work(size):
        return [
            pltpu.VMEM((size, stations), jnp.float32),
            pltpu.VMEM((size, stations), jnp.bfloat16),
            pltpu.VMEM((size // 2, CHUNK), jnp.float32),
            pltpu.VMEM((size // 2, CHUNK), jnp.float32),
        ]

    first = work(sizes[0])
    ready, inverse = pl.pallas_call(
        functools.partial(spectra_kernel, length),
        grid=(steps,),
        out_shape=[
            jax.ShapeDtypeStruct((rows, sizes[0], width), jnp.bfloat16),
            jax.ShapeDtypeStruct((1, stations), jnp.float32),
        ],
        in_specs=[
            pl.BlockSpec((1, stations, CHUNK), lambda i: (0, 0, i)),
            whole((2, half, 128)),
            whole((2, half, 128)),
            whole((1, stations)),
            whole((1, stations)),
        ],
        out_specs=[whole((rows, sizes[0], width)), whole((1, stations))],
        scratch_shapes=first[:1] + [pltpu.VMEM((stations, 128), jnp.float32)] + first[1:],
        compiler_params=pltpu.CompilerParams(vmem_limit_bytes=VMEM_BYTES),
        name="spectra",
    )(waveform, *tables, valid_mask, order)

    dma = pltpu.SemaphoreType.DMA
    chips = rows // 2
    in_vmem = pl.BlockSpec(memory_space=pltpu.VMEM)
    anywhere = pl.BlockSpec(memory_space=pl.ANY)
    row_all, col_all = pl.pallas_call(
        functools.partial(exchange_kernel, rows, cols),
        out_shape=[
            jax.ShapeDtypeStruct((cols, rows, double_bins, width), jnp.bfloat16),
            jax.ShapeDtypeStruct((cols, rows, per, double_bins, width), jnp.bfloat16),
        ],
        in_specs=[anywhere, anywhere] + [in_vmem] * 5,
        out_specs=[anywhere] * 2,
        scratch_shapes=[dma((2, 2))]
        + [dma((2, rows))] * 2
        + [dma((2, cols))] * 2
        + [dma((cols, 2))] * 4
        + [dma((2, chips))] * 4
        + [pltpu.VMEM((2, stations, CHUNK), jnp.bfloat16), dma((2,))]
        + work(sizes[1])
        + [pltpu.VMEM((rows, sizes[1], width), jnp.bfloat16)],
        compiler_params=pltpu.CompilerParams(
            collective_id=0, has_side_effects=True, vmem_limit_bytes=VMEM_BYTES
        ),
        name="exchange",
    )(ready, waveform, *tables, valid_mask, order, inverse)
    row_all = row_all.reshape(windows, double_bins, width)
    col_all = col_all.reshape(windows, per, double_bins, width)

    depth = 2 * BINS
    return pl.pallas_call(
        functools.partial(pairs_kernel, float(windows) ** (-0.5)),
        grid=(bands,),
        out_shape=jax.ShapeDtypeStruct((2, half, width, per * width), jnp.bfloat16),
        in_specs=[
            pl.BlockSpec((windows, depth, width), lambda b: (0, b, 0)),
            pl.BlockSpec((windows, per, depth, width), lambda b: (0, 0, b, 0)),
        ],
        out_specs=pl.BlockSpec(memory_space=pl.ANY),
        scratch_shapes=[
            pltpu.VMEM((2, 2, BINS, width, per * width), jnp.bfloat16),
            pltpu.SemaphoreType.DMA((2, 2, BINS)),
        ],
        compiler_params=pltpu.CompilerParams(vmem_limit_bytes=VMEM_BYTES),
        name="pairs",
    )(row_all, col_all)


def solution(mesh):
    placed = (P(("row", "col"), None, None), P(("row", "col"), None), P(), P())
    return jax.shard_map(
        functools.partial(body, mesh.shape["row"], mesh.shape["col"]),
        mesh=mesh, in_specs=placed, out_specs=P(None, None, "row", "col"), check_vma=False,
    )
```

time: 96.3 us -> 107 us (1.11)
  Pallas kernels: 93.4 us -> 104 us
    pallas_call x1, Pallas kernels: 60.9 us -> 72.6 us  [body(): pl.pallas_call(functools.partial(exchange_kernel, rows, cols), out_shape=...]
where the time goes in v5:
time: 107 us
  Pallas kernels  104 us (97%)
  other arithmetic  2.19 us (2%)
    pallas_call x1, Pallas kernels, body(): pl.pallas_call(functools.partial(exchange_kernel, rows, cols), out_shape=...  72.6 us
    pallas_call x1, Pallas kernels, body(): pl.pallas_call(functools.partial(pairs_kernel, float(windows) ** (-0.5)),...  16.4 us
    pallas_call x1, Pallas kernels, body(): pl.pallas_call(functools.partial(spectra_kernel, length), grid=(steps,),...  15.4 us

profile of v5, /device:TPU:0, one launch (start us, length us, event | category | flops | bytes accessed | tf_op | source)
XLA Modules:
  0.0 106.7 jit_solution(8758745129524783980)
XLA Ops:
  0.0 0.7 iota_add_fusion
  0.7 0.1 add.29
  0.8 1.5 %fusion.3 = (f32[2,160,128]{2,1,0:T(8,128)}, f32[2,160,128]{2,1,0:T(8,128)}) fusion(s32[2,128]{1,0:T(2,128)S(1)} %pad_add_fusion, s32[160]{0:T(256)S(1)} %add.29), kind=kLoop, calls=%fused_computation.8 | loop fusion | flops 573440 | bytes 329344 | tf_op jit(solution)/shard_map/sin | solution.py:23
  2.3 15.4 %spectra.1 = (bf16[8,160,128]{2,1,0:T(8,128)(2,1)}, f32[1,1024]{1,0:T(1,128)}) custom-call(bf16[1,1024,8192]{2,1,0:T(8,128)(2,1)} %waveform.1, f32[2,160,128]{2,1,0:T(8,128)} %get-tuple-element.14.cosines, f32[2,160,128]{2,1,0:T(8,128)} %get-tuple-element.13.sines, s32[1,1024]{1,0:T(1,128)} %mask.3, s32[1,1024]{1,0:T(1,128)} %bitcast.5), custom_call_target="tpu_custom_call" | custom-call | tf_op jit(solution)/shard_map/spectra/pallas_call | solution.py:411
  17.7 72.6 %exchange.1 = (bf16[4,8,320,128]{3,2,1,0:T(8,128)(2,1)}, bf16[4,8,2,320,128]{4,3,2,1,0:T(8,128)(2,1)}) custom-call(bf16[8,160,128]{2,1,0:T(8,128)(2,1)} %get-tuple-element.9.ready, bf16[1,1024,8192]{2,1,0:T(8,128)(2,1)} %waveform.1, f32[2,160,128]{2,1,0:T(8,128)} %get-tuple-element.14.cosines, f32[2,160,128]{2,1,0:T(8,128)} %get-tuple-element.13.sines, ...), custom_call_target="tpu_custom_call" | custom-call | tf_op jit(solution)/shard_map/exchange/pallas_call | solution.py:435
  90.3 16.4 %pairs.1 = bf16[2,160,128,256]{3,2,1,0:T(8,128)(2,1)} custom-call(bf16[32,320,128]{2,1,0:T(8,128)(2,1)} %bitcast.4, bf16[32,2,320,128]{3,2,1,0:T(8,128)(2,1)} %bitcast.3), custom_call_target="tpu_custom_call" | custom-call | tf_op jit(solution)/shard_map/pairs/pallas_call | solution.py:460
  (3 shorter events, 0.0 us)

commit v6 on v4

--- a/solution.py
+++ b/solution.py
@@ -12,6 +12,7 @@
 CHUNK = 1024
 PIECES = 2
 VIEWS = 4
+GROUP = 16
 VMEM_BYTES = 60 * 1024 * 1024
 MESH = pl.DeviceIdType.MESH
 
@@ -29,16 +30,17 @@
     length, *refs
 ):
     waves, refs = refs[:VIEWS], refs[VIEWS:]
-    cosines, sines, mask, order, out, acc, squares, white, fine_cos, fine_sin = refs
+    cosines, sines, mask, order, out, sums_of, acc, squares, white, fine_cos, fine_sin = refs
     step = pl.program_id(0)
     each = waves[0].shape[1]
     stations = each * VIEWS
     double_bins = acc.shape[0]
+    padding = sums_of.shape[1] - double_bins
     bands = double_bins // (2 * BINS)
 
     @pl.when(step == 0)
     def _():
-        acc[...] = jnp.zeros_like(acc)
+        sums_of[...] = jnp.zeros_like(sums_of)
         squares[...] = jnp.zeros_like(squares)
         for tile in range(CHUNK // 128):
             tile_cos = cosines[1, :, tile : tile + 1]
@@ -56,10 +58,11 @@
     table = jnp.concatenate(
         [real.reshape(bands, BINS, CHUNK), imag.reshape(bands, BINS, CHUNK)], axis=1
     ).reshape(double_bins, CHUNK)
+    table = jnp.concatenate([table, jnp.zeros((padding, CHUNK), jnp.bfloat16)], axis=0)
     for view, wave in enumerate(waves):
         base = view * each
-        acc[:, base : base + each] += lax.dot_general(
-            table, wave[0], (((1,), (1,)), ((), ())), preferred_element_type=jnp.float32
+        sums_of[base : base + each, :] += lax.dot_general(
+            wave[0], table, (((1,), (1,)), ((), ())), preferred_element_type=jnp.float32
         )
         for top in range(0, each, 64):
             total = squares[base + top : base + top + 64, :]
@@ -70,6 +73,7 @@
 
     @pl.when(step == pl.num_programs(0) - 1)
     def _():
+        acc[...] = sums_of[...].T[0:double_bins]
         ones = jnp.ones((8, 128), jnp.float32)
         sums = lax.dot_general(
             ones,
@@ -248,13 +252,13 @@
         to_twin(d).wait_send()
 
 
-def pairs_kernel(scaling, row_block, col_block, out, held, sems):
+def pairs_kernel(scaling, per, *refs):
+    *views, out, held, sems = refs
     step = pl.program_id(0)
     last = pl.num_programs(0) - 1
     slot = lax.rem(step, 2)
-    windows, _, width = row_block.shape
-    per = col_block.shape[1]
-    group = 16
+    group, _, width = views[0].shape
+    windows = len(views) // (1 + per) * group
     side = group * BINS
     into = lax.broadcasted_iota(jnp.int32, (side, side), 0)
     source = lax.broadcasted_iota(jnp.int32, (side, side), 1)
@@ -264,10 +268,10 @@
     regrouped = []
     for part in range(2):
         bins = slice(part * BINS, (part + 1) * BINS)
-        for first in range(0, windows, group):
-            pieces = [row_block[first : first + group, bins, :].reshape(side, width)]
-            for block in range(per):
-                pieces.append(col_block[first : first + group, block, bins, :].reshape(side, width))
+        for first in range(0, len(views), 1 + per):
+            pieces = [
+                view[:, bins, :].reshape(side, width) for view in views[first : first + 1 + per]
+            ]
             regrouped.append(
                 jnp.dot(
                     swap, jnp.concatenate(pieces, axis=1), preferred_element_type=jnp.float32
@@ -354,6 +358,7 @@
         ],
         out_specs=whole((rows, double_bins, width)),
         scratch_shapes=[
+            pltpu.VMEM((stations, pl.cdiv(double_bins, 128) * 128), jnp.float32),
             pltpu.VMEM((double_bins, stations), jnp.float32),
             pltpu.VMEM((stations, 128), jnp.float32),
             pltpu.VMEM((double_bins, stations), jnp.bfloat16),
@@ -386,12 +391,17 @@
 
     depth = 2 * BINS
     return pl.pallas_call(
-        functools.partial(pairs_kernel, float(windows) ** (-0.5)),
+        functools.partial(pairs_kernel, float(windows) ** (-0.5), per),
         grid=(bands,),
         out_shape=jax.ShapeDtypeStruct((2, half, width, per * width), jnp.bfloat16),
         in_specs=[
-            pl.BlockSpec((windows, depth, width), lambda b: (0, b, 0)),
-            pl.BlockSpec((windows, per, depth, width), lambda b: (0, 0, b, 0)),
+            spec
+            for g in range(windows // GROUP)
+            for spec in [pl.BlockSpec((GROUP, depth, width), lambda b, g=g: (g, b, 0))]
+            + [
+                pl.BlockSpec((GROUP, None, depth, width), lambda b, g=g, p=p: (g, p, b, 0))
+                for p in range(per)
+            ]
         ],
         out_specs=pl.BlockSpec(memory_space=pl.ANY),
         scratch_shapes=[
@@ -400,7 +410,7 @@
         ],
         compiler_params=pltpu.CompilerParams(vmem_limit_bytes=VMEM_BYTES),
         name="pairs",
-    )(row_all, col_all)
+    )(*([row_all] + [col_all] * per) * (windows // GROUP))
 
 
 def solution(mesh):

time: 96.3 us -> 98.3 us (1.021)
  Pallas kernels: 93.4 us -> 95.6 us
    pallas_call x1, Pallas kernels: 16.1 us -> 18.1 us  [body(): pl.pallas_call(functools.partial(spectra_kernel, length), grid=(steps,),...]
where the time goes in v6:
time: 98.3 us; the launch traced here: 97.9 us
  Pallas kernels  95.6 us (97%)
  other arithmetic  2.19 us (2%)
    pallas_call x1, Pallas kernels, body(): pl.pallas_call(functools.partial(exchange_kernel, rows, cols), out_shape=...  60.9 us
    pallas_call x1, Pallas kernels, body(): pl.pallas_call(functools.partial(spectra_kernel, length), grid=(steps,),...  18.1 us
    pallas_call x1, Pallas kernels, body(): pl.pallas_call(functools.partial(pairs_kernel, float(windows) ** (-0.5),...  16.7 us

profile of v6, /device:TPU:0, one launch (start us, length us, event | category | flops | bytes accessed | tf_op | source)
XLA Modules:
  0.0 97.9 jit_solution(377725040894120825)
XLA Ops:
  0.0 0.7 iota_add_fusion
  0.7 0.1 add.29
  0.8 1.4 %fusion.3 = (f32[2,160,128]{2,1,0:T(8,128)}, f32[2,160,128]{2,1,0:T(8,128)}) fusion(s32[2,128]{1,0:T(2,128)S(1)} %pad_add_fusion, s32[160]{0:T(256)S(1)} %add.29), kind=kLoop, calls=%fused_computation.8 | loop fusion | flops 573440 | bytes 329344 | tf_op jit(solution)/shard_map/sin | solution.py:26
  2.3 18.1 %spectra.1.white = bf16[8,320,128]{2,1,0:T(8,128)(2,1)} custom-call(bf16[1,1024,8192]{2,1,0:T(8,128)(2,1)} %refs_3_.1, bf16[1,1024,8192]{2,1,0:T(8,128)(2,1)} %refs_3_.1, bf16[1,1024,8192]{2,1,0:T(8,128)(2,1)} %refs_3_.1, bf16[1,1024,8192]{2,1,0:T(8,128)(2,1)} %refs_3_.1, f32[2,160,128]{2,1,0:T(8,128)} %get-tuple-element.10.refs_4_, ...), custom_call_target="tpu_custom_call" | custom-call | tf_op jit(solution)/shard_map/spectra/pallas_call | solution.py:345
  20.4 60.9 %exchange.1 = (bf16[4,8,320,128]{3,2,1,0:T(8,128)(2,1)}, bf16[4,8,2,320,128]{4,3,2,1,0:T(8,128)(2,1)}) custom-call(bf16[8,320,128]{2,1,0:T(8,128)(2,1)} %spectra.1.white), custom_call_target="tpu_custom_call" | custom-call | tf_op jit(solution)/shard_map/exchange/pallas_call | solution.py:374
  81.3 16.7 %pairs.1 = bf16[2,160,128,256]{3,2,1,0:T(8,128)(2,1)} custom-call(bf16[32,320,128]{2,1,0:T(8,128)(2,1)} %bitcast.7, bf16[32,2,320,128]{3,2,1,0:T(8,128)(2,1)} %bitcast.3, bf16[32,2,320,128]{3,2,1,0:T(8,128)(2,1)} %bitcast.4, bf16[32,320,128]{2,1,0:T(8,128)(2,1)} %bitcast.8, bf16[32,2,320,128]{3,2,1,0:T(8,128)(2,1)} %bitcast.5, bf16[32,2,320,128]{3,2,1,0:T(8,128)(2,1)} %bitcast.6), custom_call_target="tpu_custom_call" | custom-call | tf_op jit(solution)/shard_map/pairs/pallas_call | solution.py:393
  (3 shorter events, 0.0 us)

commit v7 on v4

--- a/solution.py
+++ b/solution.py
@@ -10,7 +10,7 @@
 
 BINS = 16
 CHUNK = 1024
-PIECES = 2
+PIECES = 4
 VIEWS = 4
 VMEM_BYTES = 60 * 1024 * 1024
 MESH = pl.DeviceIdType.MESH
@@ -58,26 +58,27 @@
     ).reshape(double_bins, CHUNK)
     for view, wave in enumerate(waves):
         base = view * each
-        acc[:, base : base + each] += lax.dot_general(
-            table, wave[0], (((1,), (1,)), ((), ())), preferred_element_type=jnp.float32
-        )
-        for top in range(0, each, 64):
-            total = squares[base + top : base + top + 64, :]
-            for tile in range(CHUNK // 128):
-                part = wave[0, top : top + 64, tile * 128 : (tile + 1) * 128].astype(jnp.float32)
-                total = total + part * part
-            squares[base + top : base + top + 64, :] = total
+        product = lax.dot_general(
+            jnp.concatenate([table, wave[0]], axis=0),
+            wave[0],
+            (((1,), (1,)), ((), ())),
+            preferred_element_type=jnp.float32,
+        )
+        acc[:, base : base + each] += product[0:double_bins]
+        squares[view] += product[double_bins:]
 
     @pl.when(step == pl.num_programs(0) - 1)
     def _():
-        ones = jnp.ones((8, 128), jnp.float32)
-        sums = lax.dot_general(
-            ones,
-            squares[...],
-            (((1,), (1,)), ((), ())),
-            precision=lax.Precision.HIGHEST,
-            preferred_element_type=jnp.float32,
-        )[0:1]
+        diagonal = lax.broadcasted_iota(jnp.int32, (each, each), 0) == lax.broadcasted_iota(
+            jnp.int32, (each, each), 1
+        )
+        sums = jnp.concatenate(
+            [
+                jnp.sum(jnp.where(diagonal, squares[view], 0.0), axis=0, keepdims=True)
+                for view in range(VIEWS)
+            ],
+            axis=1,
+        )
         inverse = 1.0 / jnp.sqrt(sums / length + 1e-06)
         valid = mask[...].astype(jnp.float32)
         for band in range(bands):
@@ -355,7 +356,7 @@
         out_specs=whole((rows, double_bins, width)),
         scratch_shapes=[
             pltpu.VMEM((double_bins, stations), jnp.float32),
-            pltpu.VMEM((stations, 128), jnp.float32),
+            pltpu.VMEM((VIEWS, stations // VIEWS, stations // VIEWS), jnp.float32),
             pltpu.VMEM((double_bins, stations), jnp.bfloat16),
             pltpu.VMEM((half, CHUNK), jnp.float32),
             pltpu.VMEM((half, CHUNK), jnp.float32),

time: 96.3 us -> 97 us (level)
  no operation moved by 1% of the time
where the time goes in v7:
time: 97 us; the launch traced here: 96.4 us
  Pallas kernels  94.1 us (97%)
  other arithmetic  2.19 us (2%)
    pallas_call x1, Pallas kernels, body(): pl.pallas_call(functools.partial(exchange_kernel, rows, cols), out_shape=...  61.2 us
    pallas_call x1, Pallas kernels, body(): pl.pallas_call(functools.partial(spectra_kernel, length), grid=(steps,),...  16.5 us
    pallas_call x1, Pallas kernels, body(): pl.pallas_call(functools.partial(pairs_kernel, float(windows) ** (-0.5)),...  16.4 us

profile of v7, /device:TPU:0, one launch (start us, length us, event | category | flops | bytes accessed | tf_op | source)
XLA Modules:
  0.0 96.4 jit_solution(4172321980257490854)
XLA Ops:
  0.0 0.7 iota_add_fusion
  0.7 0.1 add.29
  0.8 1.4 %fusion.3 = (f32[2,160,128]{2,1,0:T(8,128)}, f32[2,160,128]{2,1,0:T(8,128)}) fusion(s32[2,128]{1,0:T(2,128)S(1)} %pad_add_fusion, s32[160]{0:T(256)S(1)} %add.29), kind=kLoop, calls=%fused_computation.8 | loop fusion | flops 573440 | bytes 329344 | tf_op jit(solution)/shard_map/sin | solution.py:25
  2.3 16.5 %spectra.1.white = bf16[8,320,128]{2,1,0:T(8,128)(2,1)} custom-call(bf16[1,1024,8192]{2,1,0:T(8,128)(2,1)} %refs_3_.1, bf16[1,1024,8192]{2,1,0:T(8,128)(2,1)} %refs_3_.1, bf16[1,1024,8192]{2,1,0:T(8,128)(2,1)} %refs_3_.1, bf16[1,1024,8192]{2,1,0:T(8,128)(2,1)} %refs_3_.1, f32[2,160,128]{2,1,0:T(8,128)} %get-tuple-element.10.refs_4_, ...), custom_call_target="tpu_custom_call" | custom-call | tf_op jit(solution)/shard_map/spectra/pallas_call | solution.py:342
  18.8 61.2 %exchange.1 = (bf16[4,8,320,128]{3,2,1,0:T(8,128)(2,1)}, bf16[4,8,2,320,128]{4,3,2,1,0:T(8,128)(2,1)}) custom-call(bf16[8,320,128]{2,1,0:T(8,128)(2,1)} %spectra.1.white), custom_call_target="tpu_custom_call" | custom-call | tf_op jit(solution)/shard_map/exchange/pallas_call | solution.py:370
  79.9 16.4 %pairs.1 = bf16[2,160,128,256]{3,2,1,0:T(8,128)(2,1)} custom-call(bf16[32,320,128]{2,1,0:T(8,128)(2,1)} %bitcast.4, bf16[32,2,320,128]{3,2,1,0:T(8,128)(2,1)} %bitcast.3), custom_call_target="tpu_custom_call" | custom-call | tf_op jit(solution)/shard_map/pairs/pallas_call | solution.py:389
  (3 shorter events, 0.0 us)

commit v8 on v4

--- a/solution.py
+++ b/solution.py
@@ -9,7 +9,7 @@
 from jax.sharding import PartitionSpec as P
 
 BINS = 16
-CHUNK = 1024
+CHUNK = 2048
 PIECES = 2
 VIEWS = 4
 VMEM_BYTES = 60 * 1024 * 1024

time: 96.3 us -> 95.8 us (level)
  no operation moved by 1% of the time
where the time goes in v8:
time: 95.8 us; the launch traced here: 95.4 us
  Pallas kernels  93.1 us (97%)
  other arithmetic  2.19 us (2%)
    pallas_call x1, Pallas kernels, body(): pl.pallas_call(functools.partial(exchange_kernel, rows, cols), out_shape=...  60.8 us
    pallas_call x1, Pallas kernels, body(): pl.pallas_call(functools.partial(pairs_kernel, float(windows) ** (-0.5)),...  16.4 us
    pallas_call x1, Pallas kernels, body(): pl.pallas_call(functools.partial(spectra_kernel, length), grid=(steps,),...  15.8 us

profile of v8, /device:TPU:0, one launch (start us, length us, event | category | flops | bytes accessed | tf_op | source)
XLA Modules:
  0.0 95.4 jit_solution(9473085681551461435)
XLA Ops:
  0.0 0.7 iota_add_fusion
  0.7 0.1 add.29
  0.8 1.4 %fusion.3 = (f32[2,160,128]{2,1,0:T(8,128)}, f32[2,160,128]{2,1,0:T(8,128)}) fusion(s32[2,128]{1,0:T(2,128)S(1)} %pad_add_fusion, s32[160]{0:T(256)S(1)} %add.29), kind=kLoop, calls=%fused_computation.8 | loop fusion | flops 573440 | bytes 329344 | tf_op jit(solution)/shard_map/sin | solution.py:25
  2.3 15.8 %spectra.1.white = bf16[8,320,128]{2,1,0:T(8,128)(2,1)} custom-call(bf16[1,1024,8192]{2,1,0:T(8,128)(2,1)} %refs_3_.1, bf16[1,1024,8192]{2,1,0:T(8,128)(2,1)} %refs_3_.1, bf16[1,1024,8192]{2,1,0:T(8,128)(2,1)} %refs_3_.1, bf16[1,1024,8192]{2,1,0:T(8,128)(2,1)} %refs_3_.1, f32[2,160,128]{2,1,0:T(8,128)} %get-tuple-element.10.refs_4_, ...), custom_call_target="tpu_custom_call" | custom-call | tf_op jit(solution)/shard_map/spectra/pallas_call | solution.py:341
  18.1 60.8 %exchange.1 = (bf16[4,8,320,128]{3,2,1,0:T(8,128)(2,1)}, bf16[4,8,2,320,128]{4,3,2,1,0:T(8,128)(2,1)}) custom-call(bf16[8,320,128]{2,1,0:T(8,128)(2,1)} %spectra.1.white), custom_call_target="tpu_custom_call" | custom-call | tf_op jit(solution)/shard_map/exchange/pallas_call | solution.py:369
  78.9 16.4 %pairs.1 = bf16[2,160,128,256]{3,2,1,0:T(8,128)(2,1)} custom-call(bf16[32,320,128]{2,1,0:T(8,128)(2,1)} %bitcast.4, bf16[32,2,320,128]{3,2,1,0:T(8,128)(2,1)} %bitcast.3), custom_call_target="tpu_custom_call" | custom-call | tf_op jit(solution)/shard_map/pairs/pallas_call | solution.py:388
  (3 shorter events, 0.0 us)
